TPU v7x, 32 devices: a whole 2x2x4 slice. The times are simulated.
32 devices in a mesh: shard: 2 (over x), rep: 16 (over z, y, core).
Axes of the slice: x: 2, y: 2, z: 4, core: 2. Of those that a mesh axis runs over, the one named last changes fastest.
Arguments:
- tokens: bfloat16 [64, 1024, 576], P(('shard', 'rep')), may hold values from -6 to 6
- cotangent: bfloat16 [64, 1024, 576], P(('shard', 'rep')), may hold values from -6 to 6
- lengths: int32 [64], P(('shard', 'rep')), may hold values from 256 to 1024, as said below
- w_query: bfloat16 [576, 576], P('shard')
- w_keyval: bfloat16 [576, 2, 192], P('shard')
- w_output: bfloat16 [576, 576], P('shard')
- w_gateup: bfloat16 [576, 2, 1536], P('shard')
- w_down: bfloat16 [1536, 576], P('shard')
- gains: bfloat16 [576, 2], P('shard')
- state_query: float32 [2, 576, 576], P(None, 'shard'), as said below
- state_keyval: float32 [2, 576, 2, 192], P(None, 'shard'), as said below
- state_output: float32 [2, 576, 576], P(None, 'shard'), as said below
- state_gateup: float32 [2, 576, 2, 1536], P(None, 'shard'), as said below
- state_down: float32 [2, 1536, 576], P(None, 'shard'), as said below
- state_gains: float32 [2, 576, 2], P(None, 'shard'), as said below
Outputs:
- layer_out: bfloat16 [64, 1024, 576], P(('shard', 'rep'))
- grad_tokens: bfloat16 [64, 1024, 576], P(('shard', 'rep'))
- grad_query: float32 [576, 576], P('shard')
- grad_keyval: float32 [576, 2, 192], P('shard')
- grad_output: float32 [576, 576], P('shard')
- grad_gateup: float32 [576, 2, 1536], P('shard')
- grad_down: float32 [1536, 576], P('shard')
- grad_gains: float32 [576, 2], P('shard')
- new_state_query: float32 [2, 576, 576], P(None, 'shard')
- new_state_keyval: float32 [2, 576, 2, 192], P(None, 'shard')
- new_state_output: float32 [2, 576, 576], P(None, 'shard')
- new_state_gateup: float32 [2, 576, 2, 1536], P(None, 'shard')
- new_state_down: float32 [2, 1536, 576], P(None, 'shard')
- new_state_gains: float32 [2, 576, 2], P(None, 'shard')
- master_query: float32 [576, 576], P('shard')
- master_keyval: float32 [576, 2, 192], P('shard')
- master_output: float32 [576, 576], P('shard')
- master_gateup: float32 [576, 2, 1536], P('shard')
- master_down: float32 [1536, 576], P('shard')
- master_gains: float32 [576, 2], P('shard')
- copy_query: bfloat16 [576, 576], P('shard')
- copy_keyval: bfloat16 [576, 2, 192], P('shard')
- copy_output: bfloat16 [576, 576], P('shard')
- copy_gateup: bfloat16 [576, 2, 1536], P('shard')
- copy_down: bfloat16 [1536, 576], P('shard')
- copy_gains: bfloat16 [576, 2], P('shard')
- weight_norms: float32 [9], replicated
- update_norms: float32 [9], replicated
- trust_ratios: float32 [9], replicated
Inputs may be any that keep to these rules, and one draw needn't show every extreme that they name: Sequence s has live tokens in slots 0 to lengths[s] - 1 and padding after; some sequence has 1024 live tokens and some has 256. `state_query`: second moments (index 1 of the first dimension) are positive. `state_keyval`: second moments are positive. `state_output`: second moments are positive. `state_gateup`: second moments are positive. `state_down`: second moments are positive. `state_gains`: second moments are positive.
All inputs are finite; a program needn't handle non-finite values.
Results may differ from a plain program's by a relative error of at most 0.017.
The roundings to bfloat16 on the way count: a program that leaves them out, or rounds other values in their place, can miss the bound.
Values may be sent and summed in bfloat16 or wider, within the bound.
No kernel may reach another device: no remote copies, remote signals or barrier semaphores. Data moves between devices by JAX's collectives and lax.ppermute only.
A program may use at most 448 MiB of HBM per device.

v0:
```python
import jax
import jax.numpy as jnp
from jax import lax
from jax.sharding import PartitionSpec as P

HEAD = 64
SLOTS = 1024
MB = 2


EPSILON = 1e-05
LEARN_RATE = 0.5
STATE_DECAY = 0.5
WEIGHT_DECAY = 0.01
STACKED = (False, True, False, True, False, True)


def rotation(seq_slots, head_width):
    half_width = head_width // 2
    inverse = 10000.0 ** (-(jnp.arange(half_width, dtype=jnp.float32) * 2.0 / head_width))
    angles = jnp.arange(seq_slots, dtype=jnp.float32)[:, None] * inverse[None, :]
    cos_table = jnp.concatenate([jnp.cos(angles), jnp.cos(angles)], -1)
    sin_table = jnp.concatenate([jnp.sin(angles), jnp.sin(angles)], -1)
    return (cos_table, sin_table)


def rotate(tensor, cos_table, sin_table):
    half_width = tensor.shape[-1] // 2
    turned = jnp.concatenate([-tensor[..., half_width:], tensor[..., :half_width]], -1)
    return tensor * cos_table[:, None, :] + turned * sin_table[:, None, :]


def rotate_back(gradient, cos_table, sin_table):
    half_width = gradient.shape[-1] // 2
    moved = gradient * sin_table[:, None, :]
    turned = jnp.concatenate([moved[..., half_width:], -moved[..., :half_width]], -1)
    return gradient * cos_table[:, None, :] + turned


def allowed_mask(seq_length):
    position = jnp.arange(SLOTS)
    return (position[None, :] <= position[:, None]) & (position[None, :] < seq_length)


def masked_scores(query_rot, key_rot, seq_length):
    raw_score = jnp.einsum("qkgd,ckd->kgqc", query_rot, key_rot, preferred_element_type=jnp.float32)
    return jnp.where(allowed_mask(seq_length)[None, None], raw_score * HEAD ** (-0.5), -1e30)


def attend_forward(packed):
    query_rot, key_rot, values_in, seq_length = packed
    scores = masked_scores(query_rot, key_rot, seq_length)
    peak_score = jnp.max(scores, -1, keepdims=True)
    exponent = jnp.exp(scores - peak_score)
    denominator = jnp.sum(exponent, -1, keepdims=True)
    probs_low = (exponent / denominator).astype(jnp.bfloat16)
    mixed_out = jnp.einsum(
        "kgqc,ckd->qkgd", probs_low, values_in, preferred_element_type=jnp.float32
    )
    return (mixed_out, peak_score + jnp.log(denominator))


def attend_back(packed):
    query_rot, key_rot, values_in, grad_mixed, log_total, seq_length = packed
    scores = masked_scores(query_rot, key_rot, seq_length)
    probs = jnp.exp(scores - log_total)
    grad_values = jnp.einsum(
        "kgqc,qkgd->ckd", probs.astype(jnp.bfloat16), grad_mixed, preferred_element_type=jnp.float32
    )
    grad_probs = jnp.einsum(
        "qkgd,ckd->kgqc", grad_mixed, values_in, preferred_element_type=jnp.float32
    )
    grad_scores = (probs * (grad_probs - jnp.sum(probs * grad_probs, -1, keepdims=True))).astype(
        jnp.bfloat16
    )
    grad_query = HEAD ** (-0.5) * jnp.einsum(
        "kgqc,ckd->qkgd", grad_scores, key_rot, preferred_element_type=jnp.float32
    )
    grad_keys = HEAD ** (-0.5) * jnp.einsum(
        "kgqc,qkgd->ckd", grad_scores, query_rot, preferred_element_type=jnp.float32
    )
    return (grad_query, grad_keys, grad_values)


def norm_back(grad_normed, inputs, row_scale, gain_column):
    gain_grad = jnp.sum(grad_normed * inputs * row_scale, 0)
    scaled = grad_normed * gain_column
    inner = jnp.mean(scaled * inputs, -1, keepdims=True)
    return (gain_grad, row_scale * scaled - inputs * row_scale * row_scale * row_scale * inner)


def micro_step(gathered, tokens_part, cotangent_part, lengths_part):
    w_query, w_keyval, w_output, w_gateup, w_down, gains = gathered
    seq_count = tokens_part.shape[0]
    model_width = tokens_part.shape[-1]
    head_count = w_query.shape[-1] // HEAD
    kv_count = w_keyval.shape[-1] // HEAD
    group_size = head_count // kv_count
    gain_one = gains[:, 0].astype(jnp.float32)
    gain_two = gains[:, 1].astype(jnp.float32)
    flat_rows = tokens_part.reshape(-1, model_width).astype(jnp.float32)
    scale_one = lax.rsqrt(jnp.mean(flat_rows * flat_rows, -1, keepdims=True) + EPSILON)
    normed_one = (flat_rows * scale_one * gain_one).astype(jnp.bfloat16)
    queries = jnp.dot(normed_one, w_query, preferred_element_type=jnp.float32)
    keys_values = jnp.einsum(
        "nd,dtk->ntk", normed_one, w_keyval, preferred_element_type=jnp.float32
    )
    cos_table, sin_table = rotation(SLOTS, HEAD)
    query_rot = rotate(
        queries.reshape(seq_count, SLOTS, head_count, HEAD), cos_table, sin_table
    ).astype(jnp.bfloat16)
    query_rot = query_rot.reshape(seq_count, SLOTS, kv_count, group_size, HEAD)
    key_rot = rotate(
        keys_values[:, 0].reshape(seq_count, SLOTS, kv_count, HEAD), cos_table, sin_table
    ).astype(jnp.bfloat16)
    values_in = keys_values[:, 1].reshape(seq_count, SLOTS, kv_count, HEAD).astype(jnp.bfloat16)
    mixed_out, log_total = lax.map(attend_forward, (query_rot, key_rot, values_in, lengths_part))
    attended = mixed_out.reshape(-1, head_count * HEAD).astype(jnp.bfloat16)
    middle = flat_rows + jnp.dot(attended, w_output, preferred_element_type=jnp.float32)
    scale_two = lax.rsqrt(jnp.mean(middle * middle, -1, keepdims=True) + EPSILON)
    normed_two = (middle * scale_two * gain_two).astype(jnp.bfloat16)
    gate_up = jnp.einsum("nd,dtf->ntf", normed_two, w_gateup, preferred_element_type=jnp.float32)
    gate_lin = gate_up[:, 0]
    up_lin = gate_up[:, 1]
    sigmoid_gate = jax.nn.sigmoid(gate_lin)
    activation = gate_lin * sigmoid_gate
    hidden = (activation * up_lin).astype(jnp.bfloat16)
    result = middle + jnp.dot(hidden, w_down, preferred_element_type=jnp.float32)
    live = (jnp.arange(SLOTS)[None, :] < lengths_part[:, None]).astype(jnp.float32).reshape(-1, 1)
    grad_result = cotangent_part.reshape(-1, model_width).astype(jnp.float32) * live
    grad_low = grad_result.astype(jnp.bfloat16)
    grad_down = jnp.einsum("nf,nd->fd", hidden, grad_low, preferred_element_type=jnp.float32)
    grad_hidden = jnp.einsum("nd,fd->nf", grad_low, w_down, preferred_element_type=jnp.float32)
    grad_gate = grad_hidden * up_lin * sigmoid_gate * (1.0 + gate_lin * (1.0 - sigmoid_gate))
    grad_gu = jnp.stack([grad_gate, grad_hidden * activation], 1).astype(jnp.bfloat16)
    grad_gateup = jnp.einsum("nd,ntf->dtf", normed_two, grad_gu, preferred_element_type=jnp.float32)
    grad_two = jnp.einsum("ntf,dtf->nd", grad_gu, w_gateup, preferred_element_type=jnp.float32)
    gain_grad_two, through_two = norm_back(grad_two, middle, scale_two, gain_two)
    grad_middle = grad_result + through_two
    grad_mid_low = grad_middle.astype(jnp.bfloat16)
    grad_output = jnp.einsum(
        "nq,nd->qd", attended, grad_mid_low, preferred_element_type=jnp.float32
    )
    grad_att = jnp.einsum(
        "nd,qd->nq", grad_mid_low, w_output, preferred_element_type=jnp.float32
    ).astype(jnp.bfloat16)
    grad_att = grad_att.reshape(seq_count, SLOTS, kv_count, group_size, HEAD)
    grad_query, grad_keys, grad_values = lax.map(
        attend_back, (query_rot, key_rot, values_in, grad_att, log_total, lengths_part)
    )
    grad_q_low = rotate_back(
        grad_query.reshape(seq_count, SLOTS, head_count, HEAD), cos_table, sin_table
    ).astype(jnp.bfloat16)
    grad_q_low = grad_q_low.reshape(-1, head_count * HEAD)
    grad_k_low = (
        rotate_back(grad_keys, cos_table, sin_table)
        .astype(jnp.bfloat16)
        .reshape(-1, kv_count * HEAD)
    )
    grad_v_low = grad_values.astype(jnp.bfloat16).reshape(-1, kv_count * HEAD)
    grad_kv = jnp.stack([grad_k_low, grad_v_low], 1)
    grad_wquery = jnp.einsum(
        "nd,nq->dq", normed_one, grad_q_low, preferred_element_type=jnp.float32
    )
    grad_wkeyval = jnp.einsum(
        "nd,ntk->dtk", normed_one, grad_kv, preferred_element_type=jnp.float32
    )
    grad_one = jnp.einsum("nq,dq->nd", grad_q_low, w_query, preferred_element_type=jnp.float32)
    grad_one = grad_one + jnp.einsum(
        "ntk,dtk->nd", grad_kv, w_keyval, preferred_element_type=jnp.float32
    )
    gain_grad_one, through_one = norm_back(grad_one, flat_rows, scale_one, gain_one)
    grad_rows = grad_middle + through_one
    grad_gains = jnp.stack([gain_grad_one, gain_grad_two], 1)
    weight_grads = (grad_wquery, grad_wkeyval, grad_output, grad_gateup, grad_down, grad_gains)
    return (
        weight_grads,
        result.astype(jnp.bfloat16).reshape(tokens_part.shape),
        grad_rows.astype(jnp.bfloat16).reshape(tokens_part.shape),
    )


def matrix_squares(tensor, stacked):
    if stacked:
        return [jnp.sum(tensor[:, 0] * tensor[:, 0]), jnp.sum(tensor[:, 1] * tensor[:, 1])]
    return [jnp.sum(tensor * tensor)]


def matrix_counts(tensor, stacked):
    if stacked:
        return [tensor[:, 0].size, tensor[:, 1].size]
    return [tensor.size]


def spread_factor(factors, start, tensor, stacked):
    if stacked:
        return factors[start : start + 2].reshape((1, 2) + (1,) * (tensor.ndim - 2))
    return factors[start]


def local(
    tokens,
    cotangent,
    lengths,
    w_query,
    w_keyval,
    w_output,
    w_gateup,
    w_down,
    gains,
    state_query,
    state_keyval,
    state_output,
    state_gateup,
    state_down,
    state_gains,
):
    shards = (w_query, w_keyval, w_output, w_gateup, w_down, gains)
    states = (state_query, state_keyval, state_output, state_gateup, state_down, state_gains)
    per_micro = tokens.shape[0] // MB
    owned = None
    results_list = []
    grads_list = []
    for micro in range(MB):
        gathered = (
            lax.all_gather(shards[0], "shard", axis=0, tiled=True),
            lax.all_gather(shards[1], "shard", axis=0, tiled=True),
            lax.all_gather(shards[2], "shard", axis=0, tiled=True),
            lax.all_gather(shards[3], "shard", axis=0, tiled=True),
            lax.all_gather(shards[4], "shard", axis=0, tiled=True),
            lax.all_gather(shards[5], "shard", axis=0, tiled=True),
        )
        row_span = slice(micro * per_micro, (micro + 1) * per_micro)
        weight_grads, result, grad_rows = micro_step(
            gathered, tokens[row_span], cotangent[row_span], lengths[row_span]
        )
        results_list.append(result)
        grads_list.append(grad_rows)
        owner_part = (
            lax.psum_scatter(
                weight_grads[0].astype(jnp.bfloat16), "shard", scatter_dimension=0, tiled=True
            ).astype(jnp.float32),
            lax.psum_scatter(
                weight_grads[1].astype(jnp.bfloat16), "shard", scatter_dimension=0, tiled=True
            ).astype(jnp.float32),
            lax.psum_scatter(
                weight_grads[2].astype(jnp.bfloat16), "shard", scatter_dimension=0, tiled=True
            ).astype(jnp.float32),
            lax.psum_scatter(
                weight_grads[3].astype(jnp.bfloat16), "shard", scatter_dimension=0, tiled=True
            ).astype(jnp.float32),
            lax.psum_scatter(
                weight_grads[4].astype(jnp.bfloat16), "shard", scatter_dimension=0, tiled=True
            ).astype(jnp.float32),
            lax.psum_scatter(
                weight_grads[5].astype(jnp.bfloat16), "shard", scatter_dimension=0, tiled=True
            ).astype(jnp.float32),
        )
        owned = owner_part if owned is None else jax.tree.map(jnp.add, owned, owner_part)
    totals = lax.psum(owned, "rep")
    weights = tuple((weight.astype(jnp.float32) for weight in shards))
    shard_count = lax.axis_size("shard")
    squares_g, squares_w, entry_counts = ([], [], [])
    for weight, gradient, stacked in zip(weights, totals, STACKED):
        squares_g.extend(matrix_squares(gradient, stacked))
        squares_w.extend(matrix_squares(weight, stacked))
        entry_counts.extend([entries * shard_count for entries in matrix_counts(weight, stacked)])
    sums_g, sums_w = lax.psum((jnp.stack(squares_g), jnp.stack(squares_w)), "shard")
    grad_scale = lax.rsqrt(sums_g / jnp.array(entry_counts, dtype=jnp.float32) + 1e-06)
    firsts, seconds, directions, squares_r = ([], [], [], [])
    start = 0
    for weight, gradient, state, stacked in zip(weights, totals, states, STACKED):
        normed_grad = gradient * spread_factor(grad_scale, start, weight, stacked)
        start = start + (2 if stacked else 1)
        first_moment = STATE_DECAY * state[0] + (1.0 - STATE_DECAY) * normed_grad
        second_moment = STATE_DECAY * state[1] + (1.0 - STATE_DECAY) * normed_grad * normed_grad
        direction = first_moment / (jnp.sqrt(second_moment) + 1e-06) + WEIGHT_DECAY * weight
        firsts.append(first_moment)
        seconds.append(second_moment)
        directions.append(direction)
        squares_r.extend(matrix_squares(direction, stacked))
    sums_r = lax.psum(jnp.stack(squares_r), "shard")
    weight_norms = jnp.sqrt(sums_w)
    update_norms = jnp.sqrt(sums_r)
    trust_ratios = weight_norms * lax.rsqrt(sums_r + 1e-06)
    masters, new_states, copies = ([], [], [])
    start = 0
    for weight, direction, first_moment, second_moment, stacked in zip(
        weights, directions, firsts, seconds, STACKED
    ):
        factor = spread_factor(trust_ratios, start, weight, stacked)
        start = start + (2 if stacked else 1)
        master = weight - LEARN_RATE * factor * direction
        masters.append(master)
        copies.append(master.astype(jnp.bfloat16))
        new_states.append(jnp.stack([first_moment, second_moment]))
    layer_out = jnp.concatenate(results_list, 0)
    grad_tokens = jnp.concatenate(grads_list, 0)
    return (
        layer_out,
        grad_tokens,
        totals[0],
        totals[1],
        totals[2],
        totals[3],
        totals[4],
        totals[5],
        new_states[0],
        new_states[1],
        new_states[2],
        new_states[3],
        new_states[4],
        new_states[5],
        masters[0],
        masters[1],
        masters[2],
        masters[3],
        masters[4],
        masters[5],
        copies[0],
        copies[1],
        copies[2],
        copies[3],
        copies[4],
        copies[5],
        weight_norms,
        update_norms,
        trust_ratios,
    )


def solution(mesh):
    in_specs = (
        P(("shard", "rep"), None, None),
        P(("shard", "rep"), None, None),
        P(("shard", "rep")),
        P("shard", None),
        P("shard", None, None),
        P("shard", None),
        P("shard", None, None),
        P("shard", None),
        P("shard", None),
        P(None, "shard", None),
        P(None, "shard", None, None),
        P(None, "shard", None),
        P(None, "shard", None, None),
        P(None, "shard", None),
        P(None, "shard", None),
    )
    out_specs = (
        P(("shard", "rep"), None, None),
        P(("shard", "rep"), None, None),
        P("shard", None),
        P("shard", None, None),
        P("shard", None),
        P("shard", None, None),
        P("shard", None),
        P("shard", None),
        P(None, "shard", None),
        P(None, "shard", None, None),
        P(None, "shard", None),
        P(None, "shard", None, None),
        P(None, "shard", None),
        P(None, "shard", None),
        P("shard", None),
        P("shard", None, None),
        P("shard", None),
        P("shard", None, None),
        P("shard", None),
        P("shard", None),
        P("shard", None),
        P("shard", None, None),
        P("shard", None),
        P("shard", None, None),
        P("shard", None),
        P("shard", None),
        P(),
        P(),
        P(),
    )
    return jax.shard_map(local, mesh=mesh, in_specs=in_specs, out_specs=out_specs, check_vma=False)
```

profile of v0, /device:TPU:0, one launch (start us, length us, event | category | flops | bytes accessed | tf_op | source)
XLA Modules:
  0.0 1022.1 jit_solution(7011807464273544493)
XLA Ops:
  19.0 13.5 %all_gather.25 = bf16[576,2,192]{2,1,0:T(2,128)(2,1)S(1)} all-gather(bf16[288,2,192]{2,1,0:T(2,128)(2,1)S(1)} %copy-done.43), channel_id=1, replica_groups=mesh['shard'=2,'rep'=16] {'shard'}, dimensions={0}, use_global_device_ids=true | all-gather | bytes 663552 | tf_op jit(solution)/shard_map/all_gather | solution.py:227
  38.6 18.0 %all_gather.26 = bf16[576,576]{1,0:T(8,128)(2,1)S(1)} all-gather(bf16[288,576]{1,0:T(8,128)(2,1)S(1)} %copy-done.56), channel_id=1, replica_groups=mesh['shard'=2,'rep'=16] {'shard'}, dimensions={0}, use_global_device_ids=true | all-gather | bytes 995328 | tf_op jit(solution)/shard_map/all_gather | solution.py:226
  61.5 17.4 %all_gather.27 = bf16[576,576]{1,0:T(8,128)(2,1)} all-gather(bf16[288,576]{1,0:T(8,128)(2,1)S(1)} %copy-done.53), channel_id=1, replica_groups=mesh['shard'=2,'rep'=16] {'shard'}, dimensions={0}, use_global_device_ids=true | all-gather | bytes 995328 | tf_op jit(solution)/shard_map/all_gather | solution.py:228
  83.9 16.4 %fusion.18 = (f32[3,3,1024]{2,1,0:T(4,128)S(1)}, f32[3,1024,1024,3]{2,1,3,0:T(8,128)}) fusion(pred[1024,1024]{0,1:T(8,128)(4,1)S(1)} %fusion.37, bf16[1024,3,64,1]{0,2,3,1:T(8,128)(2,1)S(1)} %copy-done.48, bf16[1024,3,3,64]{0,3,2,1:T(8,128)(2,1)S(1)} %get-tuple-element.327), kind=kOutput, calls=%fused_computation.28 | convolution fusion | flops 1236261888 | bytes 40407040 | tf_op jit(solution)/shard_map/while/body/eval_jaxpr/qkgd,ckd->kgqc/dot_general | solution.py:46
  100.3 16.3 %fusion.6 = f32[3,3,1024]{2,1,0:T(4,128)S(1)} fusion(f32[3,3,1024]{2,1,0:T(4,128)S(1)} %get-tuple-element.366, f32[3,1024,1024,3]{2,1,3,0:T(8,128)} %get-tuple-element.367, pred[1024,1024]{0,1:T(8,128)(4,1)S(1)} %fusion.37), kind=kLoop, calls=%fused_computation.18 | loop fusion | flops 37739520 | bytes 38871040 | tf_op jit(solution)/shard_map/while/body/eval_jaxpr/reduce_sum | solution.py:55
  117.2 18.0 %fusion.141 = bf16[3,64,3,1024]{3,1,2,0:T(8,128)(2,1)} fusion(bf16[1024,3,64,1]{0,2,3,1:T(8,128)(2,1)} %bitcast.667, f32[3,3,1024]{2,1,0:T(4,128)S(1)} %fusion.6, f32[3,3,1024]{2,1,0:T(4,128)S(1)} %get-tuple-element.366, f32[3,1024,1024,3]{2,1,3,0:T(8,128)} %get-tuple-element.367, pred[1024,1024]{0,1:T(8,128)(4,1)S(1)} %fusion.37), kind=kOutput, calls=%fused_computation.219 | convolution fusion | flops 1255735296 | bytes 40443904 | tf_op jit(solution)/shard_map/while/body/eval_jaxpr/kgqc,ckd->qkgd/dot_general | solution.py:57
  139.7 15.2 %fusion.19 = (f32[3,3,1024]{2,1,0:T(4,128)S(1)}, f32[3,1024,1024,3]{2,1,3,0:T(8,128)}) fusion(pred[1024,1024]{0,1:T(8,128)(4,1)S(1)} %fusion.36, bf16[1024,3,64,1]{0,2,3,1:T(8,128)(2,1)S(1)} %copy-done.50, bf16[1024,3,3,64]{0,3,2,1:T(8,128)(2,1)S(1)} %get-tuple-element.328), kind=kOutput, calls=%fused_computation.29 | convolution fusion | flops 1236261888 | bytes 40407040 | tf_op jit(solution)/shard_map/while/body/eval_jaxpr/qkgd,ckd->kgqc/dot_general | solution.py:46
  155.0 16.3 %fusion.7 = f32[3,3,1024]{2,1,0:T(4,128)S(1)} fusion(f32[3,3,1024]{2,1,0:T(4,128)S(1)} %get-tuple-element.370, f32[3,1024,1024,3]{2,1,3,0:T(8,128)} %get-tuple-element.371, pred[1024,1024]{0,1:T(8,128)(4,1)S(1)} %fusion.36), kind=kLoop, calls=%fused_computation.19 | loop fusion | flops 37739520 | bytes 38871040 | tf_op jit(solution)/shard_map/while/body/eval_jaxpr/reduce_sum | solution.py:55
  171.4 17.1 %fusion.140 = bf16[3,64,3,1024]{3,1,2,0:T(8,128)(2,1)} fusion(bf16[1024,3,64,1]{0,2,3,1:T(8,128)(2,1)S(1)} %bitcast.669, f32[3,3,1024]{2,1,0:T(4,128)S(1)} %fusion.7, f32[3,3,1024]{2,1,0:T(4,128)S(1)} %get-tuple-element.370, f32[3,1024,1024,3]{2,1,3,0:T(8,128)} %get-tuple-element.371, pred[1024,1024]{0,1:T(8,128)(4,1)S(1)} %fusion.36), kind=kOutput, calls=%fused_computation.218 | convolution fusion | flops 1255735296 | bytes 40443904 | tf_op jit(solution)/shard_map/while/body/eval_jaxpr/kgqc,ckd->qkgd/dot_general | solution.py:57
  194.1 10.6 %fusion.237 = f32[1024,2,1536]{2,0,1:T(8,128)} fusion(bf16[576,2,1536]{2,0,1:T(8,128)(2,1)} %all-gather.4.cloned.1.call-done, f32[1024,576]{0,1:T(8,128)} %get-tuple-element.369, f32[576]{0:T(1024)S(1)} %copy-done.96, f32[1024]{0:T(1024)S(1)} %add_rsqrt_fusion.2), kind=kOutput, calls=%fused_computation.364 | convolution fusion | flops 3625648128 | bytes 18487552 | tf_op jit(solution)/shard_map/nd,dtf->ntf/dot_general | solution.py:122
  204.7 8.6 fusion.234
  213.3 10.8 %fusion.57 = (bf16[1024,1,1536]{2,0,1:T(8,128)(2,1)S(1)}, bf16[1024,1,1536]{2,0,1:T(8,128)(2,1)}) fusion(f32[1024,2,1536]{2,0,1:T(8,128)} %fusion.237, bf16[1536,576]{0,1:T(8,128)(2,1)} %all-gather.6.cloned.1.call-done, f32[1024]{0:T(1024)S(1)} %get-tuple-element.384, bf16[2,1024,576]{1,2,0:T(8,128)(2,1)} %param.17), kind=kOutput, calls=%fused_computation.93 | convolution fusion | flops 1834156032 | bytes 21827584 | tf_op jit(solution)/shard_map/nd,fd->nf/dot_general | solution.py:133
  224.2 9.6 fusion.58
  250.9 16.1 %fusion.154 = bf16[3,64,1024]{2,1,0:T(8,128)(2,1)} fusion(bf16[1024,3,3,64]{0,3,2,1:T(8,128)(2,1)S(1)} %bitcast.675, f32[3,3,1024]{2,1,0:T(4,128)S(1)} %log_add_fusion, f32[3,1024,1024,3]{2,1,3,0:T(8,128)} %get-tuple-element.371, pred[1024,1024]{0,1:T(8,128)(4,1)S(1)} %fusion.36), kind=kOutput, calls=%fused_computation.234 | convolution fusion | flops 1245904896 | bytes 40407040 | tf_op jit(solution)/shard_map/while/body/eval_jaxpr/kgqc,qkgd->ckd/dot_general | solution.py:67
  267.0 26.6 %fusion = (f32[3,3,1024]{2,1,0:T(4,128)S(1)}, f32[3,1024,1024,3]{2,1,3,0:T(8,128)}) fusion(f32[3,3,1024]{2,1,0:T(4,128)S(1)} %log_add_fusion, f32[3,1024,1024,3]{2,1,3,0:T(8,128)} %get-tuple-element.371, pred[1024,1024]{0,1:T(8,128)(4,1)S(1)} %fusion.36, bf16[1024,3,64,1]{0,2,3,1:T(8,128)(2,1)S(1)} %bitcast.670, bf16[1024,3,3,64]{0,3,2,1:T(8,128)(2,1)S(1)} %bitcast.676), kind=kOutput, calls=%fused_computation.2 | convolution fusion | flops 1255136256 | bytes 78192640 | tf_op jit(solution)/shard_map/while/body/eval_jaxpr/qkgd,ckd->kgqc/dot_general | solution.py:70
  297.6 31.5 %fusion.2 = bf16[3,3,1024,1024]{2,3,1,0:T(8,128)(2,1)} fusion(f32[3,1024,1024,3]{2,1,3,0:T(8,128)} %get-tuple-element.378, f32[3,3,1024]{2,1,0:T(4,128)S(1)} %get-tuple-element.377, f32[3,3,1024]{2,1,0:T(4,128)S(1)} %log_add_fusion, f32[3,1024,1024,3]{2,1,3,0:T(8,128)} %get-tuple-element.371, pred[1024,1024]{0,1:T(8,128)(4,1)S(1)} %fusion.36), kind=kLoop, calls=%fused_computation.4 | loop fusion | flops 56623104 | bytes 95494144 | tf_op jit(solution)/shard_map/while/body/eval_jaxpr/convert_element_type | solution.py:73
  329.2 13.2 %convolution_bitcast_fusion = f32[1024,3,64]{0,2,1:T(8,128)} fusion(bf16[1024,3,3,64]{0,3,2,1:T(8,128)(2,1)S(1)} %copy-done.16, bf16[3,3,1024,1024]{2,3,1,0:T(8,128)(2,1)} %fusion.2), kind=kOutput, calls=%fused_computation.230 | convolution fusion | flops 1207959552 | bytes 20840448 | tf_op jit(solution)/shard_map/while/body/eval_jaxpr/kgqc,qkgd->ckd/dot_general | solution.py:79
  342.4 27.0 %fusion.3 = (f32[3,3,1024]{2,1,0:T(4,128)S(1)}, f32[3,1024,1024,3]{2,1,3,0:T(8,128)}) fusion(f32[3,3,1024]{2,1,0:T(4,128)S(1)} %copy-done.85, f32[3,1024,1024,3]{2,1,3,0:T(8,128)} %get-tuple-element.367, pred[1024,1024]{0,1:T(8,128)(4,1)S(1)} %copy-done.1, bf16[1024,3,64,1]{0,2,3,1:T(8,128)(2,1)S(1)} %bitcast.668, bf16[1024,3,3,64]{0,3,2,1:T(8,128)(2,1)} %bitcast.673), kind=kOutput, calls=%fused_computation.7 | convolution fusion | flops 1255136256 | bytes 78192640 | tf_op jit(solution)/shard_map/while/body/eval_jaxpr/qkgd,ckd->kgqc/dot_general | solution.py:70
  369.4 31.7 %fusion.5 = bf16[3,3,1024,1024]{2,3,1,0:T(8,128)(2,1)} fusion(f32[3,1024,1024,3]{2,1,3,0:T(8,128)} %get-tuple-element.376, f32[3,3,1024]{2,1,0:T(4,128)S(1)} %get-tuple-element.375, f32[3,3,1024]{2,1,0:T(4,128)S(1)} %copy-done.85, f32[3,1024,1024,3]{2,1,3,0:T(8,128)} %get-tuple-element.367, pred[1024,1024]{0,1:T(8,128)(4,1)S(1)} %copy-done.1), kind=kLoop, calls=%fused_computation.9 | loop fusion | flops 56623104 | bytes 95494144 | tf_op jit(solution)/shard_map/while/body/eval_jaxpr/convert_element_type | solution.py:73
  401.1 13.2 %convolution_bitcast_fusion.1 = f32[1024,3,64]{0,2,1:T(8,128)} fusion(bf16[1024,3,3,64]{0,3,2,1:T(8,128)(2,1)S(1)} %copy-done.14, bf16[3,3,1024,1024]{2,3,1,0:T(8,128)(2,1)} %fusion.5), kind=kOutput, calls=%fused_computation.231 | convolution fusion | flops 1207959552 | bytes 20840448 | tf_op jit(solution)/shard_map/while/body/eval_jaxpr/kgqc,qkgd->ckd/dot_general | solution.py:79
  420.4 15.4 %fusion.157 = bf16[3,64,1024]{2,1,0:T(8,128)(2,1)S(1)} fusion(bf16[1024,3,3,64]{0,3,2,1:T(8,128)(2,1)S(1)} %bitcast.674, f32[3,3,1024]{2,1,0:T(4,128)S(1)} %copy-done.85, f32[3,1024,1024,3]{2,1,3,0:T(8,128)} %get-tuple-element.367, pred[1024,1024]{0,1:T(8,128)(4,1)S(1)} %copy-done.1), kind=kOutput, calls=%fused_computation.235 | convolution fusion | flops 1245904896 | bytes 40407040 | tf_op jit(solution)/shard_map/while/body/eval_jaxpr/kgqc,qkgd->ckd/dot_general | solution.py:67
  455.0 11.5 %convolution_multiply_fusion.1 = f32[3,64,3,1024]{3,1,2,0:T(8,128)} fusion(bf16[1024,3,64,1]{0,2,3,1:T(8,128)(2,1)S(1)} %copy-done.49, bf16[3,3,1024,1024]{2,3,1,0:T(8,128)(2,1)} %fusion.5), kind=kOutput, calls=%fused_computation.215 | convolution fusion | flops 1208549376 | bytes 21626880 | tf_op jit(solution)/shard_map/while/body/eval_jaxpr/kgqc,ckd->qkgd/dot_general | solution.py:76
  497.2 9.3 fusion.42
  507.2 9.2 fusion.43
  523.1 8.5 fusion.295
  548.6 20.6 %reduce-scatter.33.cloned.1.call-done = bf16[768,576]{0,1:T(8,128)(2,1)} async-done(((bf16[1536,576]{0,1:T(8,128)(2,1)}), bf16[768,576]{0,1:T(8,128)(2,1)}) %reduce-scatter.33.cloned.1.call-update) | async-done | bytes 884752 | tf_op jit(solution)/shard_map/reduce_scatter | solution.py:252
  569.3 31.0 %reduce-scatter.35.cloned.1.call-done = bf16[768,576]{0,1:T(8,128)(2,1)} async-done(((bf16[1536,576]{0,1:T(8,128)(2,1)}), bf16[768,576]{0,1:T(8,128)(2,1)}) %reduce-scatter.35.cloned.1.call-update) | async-done | bytes 884752 | tf_op jit(solution)/shard_map/reduce_scatter | solution.py:252
  603.1 47.7 %reduce-scatter.29.cloned.1.call-done = bf16[288,2,1536]{2,0,1:T(8,128)(2,1)} async-done(((bf16[576,2,1536]{2,0,1:T(8,128)(2,1)}), bf16[288,2,1536]{2,0,1:T(8,128)(2,1)}) %reduce-scatter.29.cloned.1.call-update) | async-done | bytes 1769488 | tf_op jit(solution)/shard_map/reduce_scatter | solution.py:249
  650.8 50.5 %reduce-scatter.31.cloned.1.call-done = bf16[288,2,1536]{2,0,1:T(8,128)(2,1)} async-done(((bf16[576,2,1536]{2,0,1:T(8,128)(2,1)}), bf16[288,2,1536]{2,0,1:T(8,128)(2,1)}) %reduce-scatter.31.cloned.1.call-update) | async-done | bytes 1769488 | tf_op jit(solution)/shard_map/reduce_scatter | solution.py:249
  729.0 34.4 %psum.68 = f32[288,2]{0,1:T(2,128)S(1)} all-reduce(f32[288,2]{0,1:T(2,128)S(1)} %convert_add_fusion.5), channel_id=1, replica_groups=mesh['shard'=2,'rep'=16] {'rep'}, use_global_device_ids=true, to_apply=%region_35.36 | all-reduce | flops 576 | bytes 4608 | tf_op jit(solution)/shard_map/psum | solution.py:260
  764.0 126.4 %all-reduce.4.cloned.1.call-done = (f32[288,576]{1,0:T(8,128)}, f32[288,2,192]{2,0,1:T(8,128)}, f32[288,576]{1,0:T(8,128)}, f32[288,2,1536]{2,0,1:T(8,128)}, f32[768,576]{0,1:T(8,128)}) async-done(((f32[288,576]{1,0:T(8,128)}, f32[288,2,192]{2,0,1:T(8,128)}, f32[288,576]{1,0:T(8,128)}, f32[288,2,1536]{2,0,1:T(8,128)}, f32[768,576]{0,1:T(8,128)}), (f32[288,576]{1,0:T(8,128)}, f32[288,2,192]{2,0,1:T(8,128)}, ...) | async-done | bytes 7077904 | tf_op jit(solution)/shard_map/psum | solution.py:260
  976.7 11.6 %copy.121 = f32[2,288,2,1536]{3,2,1,0:T(2,128)} copy(f32[2,288,2,1536]{3,1,2,0:T(8,128)} %pad_maximum_fusion) | data formatting | bytes 14155776
  (435 shorter events, 281.1 us)
Async XLA Ops:
  7.2 186.8 %all-gather.4.cloned.1.call-start = ((), (), s32[]{:S(2)}) async-start(), calls=%async_computation.12 | async-start | bytes 5308416 | tf_op jit(solution)/shard_map/all_gather | solution.py:229
  11.7 201.6 %all-gather.6.cloned.1.call-start = ((), (), s32[]{:S(2)}) async-start(), calls=%async_computation.13 | async-start | bytes 2654208 | tf_op jit(solution)/shard_map/all_gather | solution.py:230
  12.5 529.9 %reduce-scatter.23.cloned.1.call-start = ((), (), s32[]{:S(2)}) async-start(), calls=%async_computation.17 | async-start | bytes 884736 | tf_op jit(solution)/shard_map/reduce_scatter | solution.py:243
  18.5 39.3 %copy-start.94 = (f32[576]{0:T(1024)}, f32[576]{0:T(1024)S(1)}, u32[]{:S(2)}) copy-start(f32[576]{0:T(1024)S(1)} %get-tuple-element.249) | copy-start | bytes 6916
  34.0 22.6 %copy-start.106 = (f32[1024]{0:T(1024)}, f32[1024]{0:T(1024)S(1)}, u32[]{:S(2)}) copy-start(f32[1024]{0:T(1024)S(1)} %get-tuple-element.380) | copy-start | bytes 12292
  34.0 23.8 %copy-start.108 = (f32[1024]{0:T(1024)}, f32[1024]{0:T(1024)S(1)}, u32[]{:S(2)}) copy-start(f32[1024]{0:T(1024)S(1)} %get-tuple-element.381) | copy-start | bytes 12292
  79.6 37.7 %copy-start = (pred[1024,1024]{0,1:T(8,128)(4,1)}, pred[1024,1024]{0,1:T(8,128)(4,1)S(1)}, u32[]{:S(2)}) copy-start(pred[1024,1024]{0,1:T(8,128)(4,1)S(1)} %fusion.37) | copy-start | bytes 3145732
  83.8 16.5 %copy-start.13 = (bf16[1024,3,3,64]{0,3,2,1:T(8,128)(2,1)}, bf16[1024,3,3,64]{0,3,2,1:T(8,128)(2,1)S(1)}, u32[]{:S(2)}) copy-start(bf16[1024,3,3,64]{0,3,2,1:T(8,128)(2,1)S(1)} %get-tuple-element.327) | copy-start | bytes 3538948
  83.8 55.9 %copy-start.15 = (bf16[1024,3,3,64]{0,3,2,1:T(8,128)(2,1)}, bf16[1024,3,3,64]{0,3,2,1:T(8,128)(2,1)S(1)}, u32[]{:S(2)}) copy-start(bf16[1024,3,3,64]{0,3,2,1:T(8,128)(2,1)S(1)} %get-tuple-element.328) | copy-start | bytes 3538948
  139.7 105.7 %copy-start.98 = (f32[1024]{0:T(1024)}, f32[1024]{0:T(1024)S(1)}, u32[]{:S(2)}) copy-start(f32[1024]{0:T(1024)S(1)} %add_rsqrt_fusion.2) | copy-start | bytes 12292
  155.0 16.4 %copy-start.74 = (bf16[1024,1,192]{0,2,1:T(8,128)(2,1)S(1)}, bf16[1024,1,192]{0,2,1:T(8,128)(2,1)}, u32[]{:S(2)}) copy-start(bf16[1024,1,192]{0,2,1:T(8,128)(2,1)} %slice.587) | copy-start | bytes 1179652
  171.4 17.1 %copy-start.81 = (bf16[576,576]{1,0:T(8,128)(2,1)S(1)}, bf16[576,576]{1,0:T(8,128)(2,1)}, u32[]{:S(2)}) copy-start(bf16[576,576]{1,0:T(8,128)(2,1)} %all_gather.27) | copy-start | bytes 1990660
  192.7 52.8 %copy-start.100 = (f32[1024]{0:T(1024)}, f32[1024]{0:T(1024)S(1)}, u32[]{:S(2)}) copy-start(f32[1024]{0:T(1024)S(1)} %add_rsqrt_fusion) | copy-start | bytes 12292
  194.0 51.5 %copy-start.102 = (f32[1024]{0:T(1024)}, f32[1024]{0:T(1024)S(1)}, u32[]{:S(2)}) copy-start(f32[1024]{0:T(1024)S(1)} %get-tuple-element.385) | copy-start | bytes 12292
  194.0 51.5 %copy-start.104 = (f32[1024]{0:T(1024)}, f32[1024]{0:T(1024)S(1)}, u32[]{:S(2)}) copy-start(f32[1024]{0:T(1024)S(1)} %get-tuple-element.384) | copy-start | bytes 12292
  297.6 31.5 %copy-start.16 = (bf16[1024,3,3,64]{0,3,2,1:T(8,128)(2,1)S(1)}, bf16[1024,3,3,64]{0,3,2,1:T(8,128)(2,1)}, u32[]{:S(2)}) copy-start(bf16[1024,3,3,64]{0,3,2,1:T(8,128)(2,1)} %copy-done.15) | copy-start | bytes 3538948
  369.4 31.7 %copy-start.14 = (bf16[1024,3,3,64]{0,3,2,1:T(8,128)(2,1)S(1)}, bf16[1024,3,3,64]{0,3,2,1:T(8,128)(2,1)}, u32[]{:S(2)}) copy-start(bf16[1024,3,3,64]{0,3,2,1:T(8,128)(2,1)} %copy-done.13) | copy-start | bytes 3538948
  420.3 15.5 %copy-start.88 = (bf16[1024,3,64]{0,2,1:T(8,128)(2,1)S(1)}, bf16[1024,3,64]{0,2,1:T(8,128)(2,1)}, u32[]{:S(2)}) copy-start(bf16[1024,3,64]{0,2,1:T(8,128)(2,1)} %get-tuple-element.339) | copy-start | bytes 1179652
  420.3 122.1 %reduce-scatter.21.cloned.1.call-start = ((), (), s32[]{:S(2)}) async-start(), calls=%async_computation.16 | async-start | bytes 884736 | tf_op jit(solution)/shard_map/reduce_scatter | solution.py:243
  442.3 102.1 %reduce-scatter.25.cloned.1.call-start = ((), (), s32[]{:S(2)}) async-start(), calls=%async_computation.18 | async-start | bytes 1105920 | tf_op jit(solution)/shard_map/reduce_scatter | solution.py:246
  450.9 93.4 %reduce-scatter.27.cloned.1.call-start = ((), (), s32[]{:S(2)}) async-start(), calls=%async_computation.19 | async-start | bytes 1105920 | tf_op jit(solution)/shard_map/reduce_scatter | solution.py:246
  466.5 79.9 %reduce-scatter.19.cloned.1.call-start = ((), (), s32[]{:S(2)}) async-start(), calls=%async_computation.15 | async-start | bytes 1105920 | tf_op jit(solution)/shard_map/reduce_scatter | solution.py:240
  476.4 70.0 %reduce-scatter.17.cloned.1.call-start = ((), (), s32[]{:S(2)}) async-start(), calls=%async_computation.14 | async-start | bytes 1105920 | tf_op jit(solution)/shard_map/reduce_scatter | solution.py:240
  480.1 89.1 %reduce-scatter.33.cloned.1.call-start = ((), (), s32[]{:S(2)}) async-start(), calls=%async_computation.22 | async-start | bytes 2654208 | tf_op jit(solution)/shard_map/reduce_scatter | solution.py:252
  488.6 111.8 %reduce-scatter.35.cloned.1.call-start = ((), (), s32[]{:S(2)}) async-start(), calls=%async_computation.23 | async-start | bytes 2654208 | tf_op jit(solution)/shard_map/reduce_scatter | solution.py:252
  497.2 153.7 %reduce-scatter.29.cloned.1.call-start = ((), (), s32[]{:S(2)}) async-start(), calls=%async_computation.20 | async-start | bytes 5308416 | tf_op jit(solution)/shard_map/reduce_scatter | solution.py:249
  506.5 194.8 %reduce-scatter.31.cloned.1.call-start = ((), (), s32[]{:S(2)}) async-start(), calls=%async_computation.21 | async-start | bytes 5308416 | tf_op jit(solution)/shard_map/reduce_scatter | solution.py:249
  516.5 210.5 %reduce-scatter.37.cloned.1.call-start = ((), (), s32[]{:S(2)}) async-start(), calls=%async_computation.24 | async-start | bytes 221184
  541.1 186.8 %reduce-scatter.39.cloned.1.call-start = ((), (), s32[]{:S(2)}) async-start(), calls=%async_computation.25 | async-start | bytes 221184
  542.1 348.3 %all-reduce.4.cloned.1.call-start = ((), (), s32[]{:S(2)}) async-start(), calls=%async_computation.26 | async-start | bytes 14745600 | tf_op jit(solution)/shard_map/psum | solution.py:260
  763.3 155.2 %copy-start.90 = (f32[288,2]{0,1:T(2,128)}, f32[288,2]{0,1:T(2,128)S(1)}, u32[]{:S(2)}) copy-start(f32[288,2]{0,1:T(2,128)S(1)} %psum.68) | copy-start | bytes 6916
  976.7 16.9 %copy-start.8 = (bf16[288,2,1536]{2,1,0:T(2,128)(2,1)S(1)}, bf16[288,2,1536]{2,1,0:T(2,128)(2,1)}, u32[]{:S(2)}) copy-start(bf16[288,2,1536]{2,1,0:T(2,128)(2,1)} %param.22) | copy-start | bytes 5308420
  (109 other events, 551.5 us)
Sparse Core Ops, SparseCore 0:
  11.8 69.6 all-gather.3
  83.1 30.9 all-gather.5
  420.4 16.8 reduce-scatter.22
  442.4 16.8 reduce-scatter.20
  462.0 16.8 reduce-scatter.24
  481.7 16.8 reduce-scatter.26
  501.4 16.8 reduce-scatter.18
  521.2 16.8 reduce-scatter.16
  541.0 28.2 reduce-scatter.32
  572.1 28.2 reduce-scatter.34
  603.2 47.6 reduce-scatter.28
  653.6 47.6 reduce-scatter.30
  704.1 10.4 reduce-scatter.36
  717.2 10.4 reduce-scatter.38
  733.6 156.6 all-reduce.3
where the time goes:
time: 1030 us; the launch traced here: 1020 us
  matrix products  341 us (33%)
  waiting for transfers between devices  277 us (27%)
  other arithmetic  202 us (20%)
  blocking collectives  99.5 us (10%)
  local copies, waits for them, and re-layouts  83 us (8%)
  between operations  17.8 us (2%)
    psum x1, waiting for transfers between devices, local(): totals = lax.psum(owned, 'rep')  126 us
    reduce_scatter x2, waiting for transfers between devices, local(): lax.psum_scatter(weight_grads[3].astype(jnp.bfloat16), 'shard', scatter_d...  98.2 us
    convert_element_type x2, other arithmetic, attend_back(): (probs * (grad_probs - jnp.sum(probs * grad_probs, -1, keepdims=True))).a...  63.2 us
    dot_general x2, matrix products, attend_back(): jnp.einsum('qkgd,ckd->kgqc', grad_mixed, values_in, preferred_element_typ...  53.6 us
    reduce_scatter x2, waiting for transfers between devices, local(): lax.psum_scatter(weight_grads[4].astype(jnp.bfloat16), 'shard', scatter_d...  51.7 us
    unnamed x268, local copies, waits for them, and re-layouts  49.9 us
    dot_general x2, matrix products, attend_forward(): jnp.einsum('kgqc,ckd->qkgd', probs_low, values_in, preferred_element_type...  35.1 us
    psum x1, blocking collectives, local(): totals = lax.psum(owned, 'rep')  34.4 us
  transfers between devices with their start and end apart: 15, of which 5 were waited for; matrix products, arithmetic and copies ran while one was open for 29% of the time, Pallas kernels for 0%

commit v1 on v0

v1 whole, which is shorter than its diff:
```python
import functools
import math
import jax
import jax.numpy as jnp
import numpy as np
from jax import lax
from jax.experimental import pallas as pl
from jax.experimental.pallas import tpu as pltpu
from jax.sharding import PartitionSpec as P

HEAD = 64
SLOTS = 1024
GROUP = 3
EPSILON = 1e-05
NEG = -1e30
COEF = (HEAD ** -0.5) * math.log2(math.e)
BF = jnp.bfloat16
F32 = jnp.float32
NN = (((1,), (0,)), ((), ()))
NT = (((1,), (1,)), ((), ()))
TN = (((0,), (0,)), ((), ()))


def dot(a, b, dims=NN):
    return lax.dot_general(a, b, dims, preferred_element_type=F32)


def tables():
    half = HEAD // 2
    inverse = np.float32(10000.0) ** (-(np.arange(half, dtype=np.float32) * np.float32(2.0) / np.float32(HEAD)))
    angles = inverse.astype(np.float32)[:, None] * np.arange(SLOTS, dtype=np.float32)[None, :]
    return np.cos(angles).astype(np.float32), np.sin(angles).astype(np.float32)


def pre_kernel(x_ref, gain_ref, w_ref, cos_ref, sin_ref, out_ref, *, n_rot):
    x = x_ref[0].astype(F32)
    scale = lax.rsqrt(jnp.mean(x * x, 0, keepdims=True) + EPSILON)
    normed = (x * scale * gain_ref[...]).astype(BF)
    full = dot(w_ref[...], normed, TN)
    cos, sin = cos_ref[...], sin_ref[...]
    half = HEAD // 2
    for head in range(n_rot):
        one = full[head * HEAD : head * HEAD + half]
        two = full[head * HEAD + half : (head + 1) * HEAD]
        out_ref[0, head * HEAD : head * HEAD + half, :] = (one * cos - two * sin).astype(BF)
        out_ref[0, head * HEAD + half : (head + 1) * HEAD, :] = (two * cos + one * sin).astype(BF)
    out_ref[0, n_rot * HEAD :, :] = full[n_rot * HEAD :].astype(BF)


def pre(x_t, gain, w_qkv, cos, sin, rows=512):
    seqs, width, slots = x_t.shape
    total = w_qkv.shape[1]
    n_rot = 12
    return pl.pallas_call(
        functools.partial(pre_kernel, n_rot=n_rot),
        grid=(seqs, slots // rows),
        in_specs=[
            pl.BlockSpec((1, width, rows), lambda s, r: (s, 0, r)),
            pl.BlockSpec((width, 1), lambda s, r: (0, 0)),
            pl.BlockSpec((width, total), lambda s, r: (0, 0)),
            pl.BlockSpec((HEAD // 2, rows), lambda s, r: (0, r)),
            pl.BlockSpec((HEAD // 2, rows), lambda s, r: (0, r)),
        ],
        out_specs=pl.BlockSpec((1, total, rows), lambda s, r: (s, 0, r)),
        out_shape=jax.ShapeDtypeStruct((seqs, total, slots), BF),
        compiler_params=pltpu.CompilerParams(vmem_limit_bytes=40 << 20),
        name="pre_attention",
    )(x_t, gain, w_qkv, cos, sin)


def key_rows(k_t, length):
    slots = k_t.shape[1]
    col = lax.broadcasted_iota(jnp.int32, (HEAD, slots), 1)
    row = lax.broadcasted_iota(jnp.int32, (HEAD, slots), 0)
    bias = jnp.where((row == 0) & (col >= length), NEG, 0.0).astype(BF)
    return jnp.concatenate([k_t, bias], 0).T


def ones_rows(n):
    row = lax.broadcasted_iota(jnp.int32, (HEAD, n), 0)
    return jnp.where(row == 0, 1.0, 0.0).astype(BF)


def causal_tile(n):
    return lax.broadcasted_iota(jnp.int32, (n, n), 0) <= lax.broadcasted_iota(jnp.int32, (n, n), 1)


def att_fwd_kernel(len_ref, q_ref, k_ref, v_ref, out_ref, lse_ref, *, blk):
    length = len_ref[pl.program_id(0)]
    keys = key_rows(k_ref[0], length)
    v_t = v_ref[0]
    slots = v_t.shape[1]
    ones = ones_rows(blk)
    keep = causal_tile(blk)
    for qi in range(slots // blk):
        cols = slice(qi * blk, (qi + 1) * blk)
        span = (qi + 1) * blk
        for head in range(GROUP):
            rows = slice(head * HEAD, (head + 1) * HEAD)
            q_t = jnp.concatenate([q_ref[0, rows, cols], ones], 0)
            s = dot(keys[:span], q_t)
            last = jnp.where(keep, s[qi * blk :], NEG)
            s = last if qi == 0 else jnp.concatenate([s[: qi * blk], last], 0)
            peak = jnp.max(s, 0, keepdims=True)
            p = jnp.exp2(s * COEF - peak * COEF)
            denom = jnp.sum(p, 0, keepdims=True)
            o = dot(v_t[:, :span], p.astype(BF))
            out_ref[0, rows, cols] = (o * (1.0 / denom)).astype(BF)
            lse_ref[0, 0, head : head + 1, cols] = peak * COEF + jnp.log2(denom)


def att_fwd(qkv_t, lengths, blk=256):
    seqs, total, slots = qkv_t.shape
    kv = total // (HEAD * (GROUP + 2))
    qh = kv * GROUP
    return pl.pallas_call(
        functools.partial(att_fwd_kernel, blk=blk),
        grid_spec=pltpu.PrefetchScalarGridSpec(
            num_scalar_prefetch=1,
            grid=(seqs, kv),
            in_specs=[
                pl.BlockSpec((1, GROUP * HEAD, slots), lambda s, g, n: (s, g, 0)),
                pl.BlockSpec((1, HEAD, slots), lambda s, g, n: (s, qh + g, 0)),
                pl.BlockSpec((1, HEAD, slots), lambda s, g, n: (s, qh + kv + g, 0)),
            ],
            out_specs=[
                pl.BlockSpec((1, GROUP * HEAD, slots), lambda s, g, n: (s, g, 0)),
                pl.BlockSpec((1, 1, GROUP, slots), lambda s, g, n: (s, g, 0, 0)),
            ],
        ),
        out_shape=[
            jax.ShapeDtypeStruct((seqs, qh * HEAD, slots), BF),
            jax.ShapeDtypeStruct((seqs, kv, GROUP, slots), F32),
        ],
        compiler_params=pltpu.CompilerParams(vmem_limit_bytes=40 << 20),
        name="attention_forward",
    )(lengths, qkv_t, qkv_t, qkv_t)


def rope_back(g, cos, sin):
    half = HEAD // 2
    one, two = g[:half], g[half:]
    return jnp.concatenate([one * cos + two * sin, two * cos - one * sin], 0)


def att_bwd_kernel(len_ref, q_ref, k_ref, v_ref, go_ref, o_ref, lse_ref, cos_ref, sin_ref, dq_ref, dk_ref, dv_ref, dk_s, dv_s, *, blk):
    length = len_ref[pl.program_id(0)]
    k_t = k_ref[0]
    keys = key_rows(k_t, length)
    vals = v_ref[0].T
    slots = k_t.shape[1]
    ones = ones_rows(blk)
    keep = causal_tile(blk)
    factor = HEAD ** -0.5
    dk_s[...] = jnp.zeros_like(dk_s)
    dv_s[...] = jnp.zeros_like(dv_s)
    for qi in range(slots // blk):
        cols = slice(qi * blk, (qi + 1) * blk)
        span = (qi + 1) * blk

        @pl.when(qi * blk < length)
        def _():
            for head in range(GROUP):
                rows = slice(head * HEAD, (head + 1) * HEAD)
                q_raw = q_ref[0, rows, cols]
                q_t = jnp.concatenate([q_raw, ones], 0)
                go = go_ref[0, rows, cols]
                delta = jnp.sum(go.astype(F32) * o_ref[0, rows, cols].astype(F32), 0, keepdims=True)
                s = dot(keys[:span], q_t)
                last = jnp.where(keep, s[qi * blk :], NEG)
                s = last if qi == 0 else jnp.concatenate([s[: qi * blk], last], 0)
                p = jnp.exp2(s * COEF - lse_ref[0, 0, head : head + 1, cols])
                dp = dot(vals[:span], go)
                ds = (p * (dp - delta)).astype(BF)
                dv_s[:span] += dot(p.astype(BF), go, NT)
                dk_s[:span] += dot(ds, q_raw, NT)
                dq = dot(k_t[:, :span], ds) * factor
                dq_ref[0, rows, cols] = rope_back(dq, cos_ref[:, cols], sin_ref[:, cols]).astype(BF)

        @pl.when(qi * blk >= length)
        def _():
            dq_ref[0, :, cols] = jnp.zeros((GROUP * HEAD, blk), BF)

    dk = dk_s[...].T * factor
    dk_ref[0] = rope_back(dk, cos_ref[...], sin_ref[...]).astype(BF)
    dv_ref[0] = dv_s[...].T.astype(BF)


def att_bwd(qkv_t, go_t, o_t, lse, lengths, cos, sin, blk=256):
    seqs, total, slots = qkv_t.shape
    kv = total // (HEAD * (GROUP + 2))
    qh = kv * GROUP
    return pl.pallas_call(
        functools.partial(att_bwd_kernel, blk=blk),
        grid_spec=pltpu.PrefetchScalarGridSpec(
            num_scalar_prefetch=1,
            grid=(seqs, kv),
            in_specs=[
                pl.BlockSpec((1, GROUP * HEAD, slots), lambda s, g, n: (s, g, 0)),
                pl.BlockSpec((1, HEAD, slots), lambda s, g, n: (s, qh + g, 0)),
                pl.BlockSpec((1, HEAD, slots), lambda s, g, n: (s, qh + kv + g, 0)),
                pl.BlockSpec((1, GROUP * HEAD, slots), lambda s, g, n: (s, g, 0)),
                pl.BlockSpec((1, GROUP * HEAD, slots), lambda s, g, n: (s, g, 0)),
                pl.BlockSpec((1, 1, GROUP, slots), lambda s, g, n: (s, g, 0, 0)),
                pl.BlockSpec((HEAD // 2, slots), lambda s, g, n: (0, 0)),
                pl.BlockSpec((HEAD // 2, slots), lambda s, g, n: (0, 0)),
            ],
            out_specs=[
                pl.BlockSpec((1, GROUP * HEAD, slots), lambda s, g, n: (s, g, 0)),
                pl.BlockSpec((1, HEAD, slots), lambda s, g, n: (s, g, 0)),
                pl.BlockSpec((1, HEAD, slots), lambda s, g, n: (s, g, 0)),
            ],
            scratch_shapes=[pltpu.VMEM((slots, HEAD), F32), pltpu.VMEM((slots, HEAD), F32)],
        ),
        out_shape=[
            jax.ShapeDtypeStruct((seqs, qh * HEAD, slots), BF),
            jax.ShapeDtypeStruct((seqs, kv * HEAD, slots), BF),
            jax.ShapeDtypeStruct((seqs, kv * HEAD, slots), BF),
        ],
        compiler_params=pltpu.CompilerParams(vmem_limit_bytes=40 << 20),
        name="attention_backward",
    )(lengths, qkv_t, qkv_t, qkv_t, go_t, o_t, lse, cos, sin)


def ffn_kernel(len_ref, x_ref, att_ref, ct_ref, gain_ref, wo_ref, wgu_ref, wdt_ref,
               out_ref, gmid_ref, gatt_ref, ggain_ref, gwo_ref, gwgu_ref, gwd_ref,
               wot_s, wgut_s, wd_s, awo, awgu, awd, res_s, gtwo_s, *, rows, chunk):
    seq, blk = pl.program_id(0), pl.program_id(1)
    first = (seq == 0) & (blk == 0)
    last = (seq == pl.num_programs(0) - 1) & (blk == pl.num_programs(1) - 1)
    ff = wdt_ref.shape[1]
    length = len_ref[seq]

    @pl.when(first)
    def _():
        wot_s[...] = wo_ref[...].T
        awo[...] = jnp.zeros_like(awo)
        ggain_ref[...] = jnp.zeros_like(ggain_ref)

        def tr(c, _):
            at = pl.multiple_of(c * chunk, chunk)
            wgut_s[pl.ds(at, chunk), :] = wgu_ref[:, pl.ds(at, chunk)].T
            at2 = pl.multiple_of(ff + c * chunk, chunk)
            wgut_s[pl.ds(at2, chunk), :] = wgu_ref[:, pl.ds(at2, chunk)].T
            wd_s[pl.ds(at, chunk), :] = wdt_ref[:, pl.ds(at, chunk)].T
            awgu[:, pl.ds(at, chunk)] = jnp.zeros((awgu.shape[0], chunk), F32)
            awgu[:, pl.ds(at2, chunk)] = jnp.zeros((awgu.shape[0], chunk), F32)
            awd[:, pl.ds(at, chunk)] = jnp.zeros((awd.shape[0], chunk), F32)
            return 0

        lax.fori_loop(0, ff // chunk, tr, 0)

    att = att_ref[0]
    middle = x_ref[0].astype(F32) + dot(wot_s[...], att)
    scale = lax.rsqrt(jnp.mean(middle * middle, 0, keepdims=True) + EPSILON)
    gain = gain_ref[...]
    normed = (middle * scale * gain).astype(BF)
    slot = blk * rows + lax.broadcasted_iota(jnp.int32, (1, rows), 1)
    g_res = jnp.where(slot < length, ct_ref[0].astype(F32), 0.0)
    g_low = g_res.astype(BF)
    res_s[...] = middle
    gtwo_s[...] = jnp.zeros_like(gtwo_s)

    def step(c, _):
        at = pl.multiple_of(c * chunk, chunk)
        at2 = pl.multiple_of(ff + c * chunk, chunk)
        gate = dot(wgut_s[pl.ds(at, chunk), :], normed)
        up = dot(wgut_s[pl.ds(at2, chunk), :], normed)
        sig = 1.0 / (1.0 + jnp.exp(-gate))
        act = gate * sig
        hidden = (act * up).astype(BF)
        res_s[...] += dot(wdt_ref[:, pl.ds(at, chunk)], hidden)
        g_hid = dot(wd_s[pl.ds(at, chunk), :], g_low)
        g_gate = (g_hid * up * (sig + act * (1.0 - sig))).astype(BF)
        g_up = (g_hid * act).astype(BF)
        gtwo_s[...] += dot(wgu_ref[:, pl.ds(at, chunk)], g_gate) + dot(wgu_ref[:, pl.ds(at2, chunk)], g_up)
        awd[:, pl.ds(at, chunk)] += dot(g_low, hidden, NT)
        awgu[:, pl.ds(at, chunk)] += dot(normed, g_gate, NT)
        awgu[:, pl.ds(at2, chunk)] += dot(normed, g_up, NT)
        return 0

    lax.fori_loop(0, ff // chunk, step, 0)
    out_ref[0] = res_s[...].astype(BF)
    g_two = gtwo_s[...]
    ggain_ref[...] += jnp.sum(g_two * middle * scale, 1, keepdims=True)
    e = g_two * gain
    inner = jnp.mean(e * middle, 0, keepdims=True)
    g_mid = g_res + (scale * e - middle * (scale * scale * scale * inner))
    gmid_ref[0] = g_mid
    g_mid_low = g_mid.astype(BF)
    gatt_ref[0] = dot(wo_ref[...], g_mid_low).astype(BF)
    awo[...] += dot(att, g_mid_low, NT)

    @pl.when(last)
    def _():
        gwo_ref[...] = awo[...].astype(BF)

        def wr(c, _):
            at = pl.multiple_of(c * chunk, chunk)
            at2 = pl.multiple_of(ff + c * chunk, chunk)
            gwgu_ref[:, pl.ds(at, chunk)] = awgu[:, pl.ds(at, chunk)].astype(BF)
            gwgu_ref[:, pl.ds(at2, chunk)] = awgu[:, pl.ds(at2, chunk)].astype(BF)
            gwd_ref[:, pl.ds(at, chunk)] = awd[:, pl.ds(at, chunk)].astype(BF)
            return 0

        lax.fori_loop(0, ff // chunk, wr, 0)


def ffn(x_t, att_t, ct_t, gain, w_out, w_gu, w_down_t, lengths, rows=512, chunk=256):
    seqs, width, slots = x_t.shape
    ff = w_down_t.shape[1]
    tok = pl.BlockSpec((1, width, rows), lambda s, r, n: (s, 0, r))

    def whole(shape):
        return pl.BlockSpec(shape, lambda s, r, n: (0,) * len(shape), pipeline_mode=pl.Buffered(1))

    def whole_out(shape):
        return pl.BlockSpec(shape, lambda s, r, n: (0,) * len(shape))

    return pl.pallas_call(
        functools.partial(ffn_kernel, rows=rows, chunk=chunk),
        grid_spec=pltpu.PrefetchScalarGridSpec(
            num_scalar_prefetch=1,
            grid=(seqs, slots // rows),
            in_specs=[tok, tok, tok, whole((width, 1)), whole(w_out.shape), whole(w_gu.shape), whole(w_down_t.shape)],
            out_specs=[tok, tok, tok, whole_out((width, 1)), whole_out(w_out.shape), whole_out(w_gu.shape), whole_out(w_down_t.shape)],
            scratch_shapes=[
                pltpu.VMEM((width, width), BF),
                pltpu.VMEM((2 * ff, width), BF),
                pltpu.VMEM((ff, width), BF),
                pltpu.VMEM((width, width), F32),
                pltpu.VMEM((width, 2 * ff), F32),
                pltpu.VMEM((width, ff), F32),
                pltpu.VMEM((width, rows), F32),
                pltpu.VMEM((width, rows), F32),
            ],
        ),
        out_shape=[
            jax.ShapeDtypeStruct(x_t.shape, BF),
            jax.ShapeDtypeStruct(x_t.shape, F32),
            jax.ShapeDtypeStruct(x_t.shape, BF),
            jax.ShapeDtypeStruct((width, 1), F32),
            jax.ShapeDtypeStruct(w_out.shape, BF),
            jax.ShapeDtypeStruct(w_gu.shape, BF),
            jax.ShapeDtypeStruct(w_down_t.shape, BF),
        ],
        compiler_params=pltpu.CompilerParams(vmem_limit_bytes=60 << 20),
        name="feed_forward",
    )(lengths, x_t, att_t, ct_t, gain, w_out, w_gu, w_down_t)


def post_kernel(x_ref, gq_ref, gk_ref, gv_ref, gmid_ref, gain_ref, w_ref, out_ref, ggain_ref, gw_ref, acc, *, nq, nk):
    seq, blk = pl.program_id(0), pl.program_id(1)
    first = (seq == 0) & (blk == 0)
    last = (seq == pl.num_programs(0) - 1) & (blk == pl.num_programs(1) - 1)

    @pl.when(first)
    def _():
        acc[...] = jnp.zeros_like(acc)
        ggain_ref[...] = jnp.zeros_like(ggain_ref)

    x = x_ref[0].astype(F32)
    scale = lax.rsqrt(jnp.mean(x * x, 0, keepdims=True) + EPSILON)
    gain = gain_ref[...]
    normed = (x * scale * gain).astype(BF)
    g = jnp.concatenate([gq_ref[0], gk_ref[0], gv_ref[0]], 0)
    g_one = dot(w_ref[...], g)
    acc[...] += dot(normed, g, NT)
    ggain_ref[...] += jnp.sum(g_one * x * scale, 1, keepdims=True)
    e = g_one * gain
    inner = jnp.mean(e * x, 0, keepdims=True)
    out_ref[0] = (gmid_ref[0] + (scale * e - x * (scale * scale * scale * inner))).astype(BF)

    @pl.when(last)
    def _():
        gw_ref[...] = acc[...].astype(BF)


def post(x_t, gq, gk, gv, gmid, gain, w_qkv, rows=512):
    seqs, width, slots = x_t.shape
    nq, nk, total = gq.shape[1], gk.shape[1], w_qkv.shape[1]
    tok = lambda n: pl.BlockSpec((1, n, rows), lambda s, r: (s, 0, r))
    whole = lambda shape: pl.BlockSpec(shape, lambda s, r: (0,) * len(shape))
    return pl.pallas_call(
        functools.partial(post_kernel, nq=nq, nk=nk),
        grid=(seqs, slots // rows),
        in_specs=[tok(width), tok(nq), tok(nk), tok(nk), tok(width), whole((width, 1)), whole(w_qkv.shape)],
        out_specs=[tok(width), whole((width, 1)), whole(w_qkv.shape)],
        out_shape=[
            jax.ShapeDtypeStruct(x_t.shape, BF),
            jax.ShapeDtypeStruct((width, 1), F32),
            jax.ShapeDtypeStruct(w_qkv.shape, BF),
        ],
        scratch_shapes=[pltpu.VMEM(w_qkv.shape, F32)],
        compiler_params=pltpu.CompilerParams(vmem_limit_bytes=40 << 20),
        name="post_attention",
    )(x_t, gq, gk, gv, gmid, gain, w_qkv)


LEARN_RATE = 0.5
STATE_DECAY = 0.5
WEIGHT_DECAY = 0.01
STACKED = (False, True, False, True, False, True)


def swap(v, axis, bit):
    return lax.ppermute(v, axis, [(i, i ^ (1 << bit)) for i in range(lax.axis_size(axis))])


def bit_of(axis, bit):
    return (lax.axis_index(axis) >> bit) & 1


def scatter_step(v, dim, axis, bit):
    half = v.shape[dim] // 2
    mine = bit_of(axis, bit)
    send = lax.dynamic_slice_in_dim(v, (1 - mine) * half, half, dim)
    keep = lax.dynamic_slice_in_dim(v, mine * half, half, dim)
    got = swap(send, axis, bit)
    return (keep.astype(F32) + got.astype(F32)).astype(BF)


def gather_step(v, dim, axis, bit):
    got = swap(v, axis, bit)
    mine = bit_of(axis, bit)
    return jnp.where(mine == 0, jnp.concatenate([v, got], dim), jnp.concatenate([got, v], dim))


def reduce_all(v, x_dim, dims):
    bits = (lax.axis_size("rep") - 1).bit_length()
    v = scatter_step(v, dims[0], "rep", 0)
    v = scatter_step(v, x_dim, "shard", 0)
    for b in range(1, bits):
        v = scatter_step(v, dims[b], "rep", b)
    for b in range(bits - 1, -1, -1):
        v = gather_step(v, dims[b], "rep", b)
    return v


def reduce_small(v):
    bits = (lax.axis_size("rep") - 1).bit_length()
    half = v.shape[0] // 2
    mine = bit_of("shard", 0)
    got = swap(lax.dynamic_slice_in_dim(v, (1 - mine) * half, half, 0), "shard", 0)
    v = lax.dynamic_slice_in_dim(v, mine * half, half, 0) + got
    for b in range(bits):
        v = v + swap(v, "rep", b)
    return v


def matrix_squares(tensor, stacked):
    if stacked:
        return [jnp.sum(tensor[:, 0] * tensor[:, 0]), jnp.sum(tensor[:, 1] * tensor[:, 1])]
    return [jnp.sum(tensor * tensor)]


def matrix_counts(tensor, stacked):
    if stacked:
        return [tensor[:, 0].size, tensor[:, 1].size]
    return [tensor.size]


def spread_factor(factors, start, tensor, stacked):
    if stacked:
        return factors[start : start + 2].reshape((1, 2) + (1,) * (tensor.ndim - 2))
    return factors[start]


def local(
    tokens, cotangent, lengths,
    w_query, w_keyval, w_output, w_gateup, w_down, gains,
    state_query, state_keyval, state_output, state_gateup, state_down, state_gains,
):
    width, ff = w_query.shape[0] * 2, w_gateup.shape[-1]
    nq, nkv = w_query.shape[1], w_keyval.shape[-1]
    gather = lambda v, dim: lax.all_gather(v, "shard", axis=dim, tiled=True)
    x_t, ct_t = jnp.swapaxes(tokens, 1, 2), jnp.swapaxes(cotangent, 1, 2)
    w_qkv = gather(jnp.concatenate([w_query, w_keyval.reshape(-1, 2 * nkv)], 1), 0)
    g_all = gather(gains, 0).astype(F32)
    w_o = gather(w_output, 0)
    w_gu = gather(w_gateup.reshape(-1, 2 * ff), 0)
    w_dt = gather(w_down.T, 1)
    gain_one, gain_two = g_all[:, :1], g_all[:, 1:]
    cos, sin = (jnp.asarray(t) for t in tables())
    qkv_t = pre(x_t, gain_one, w_qkv, cos, sin)
    att_t, lse = att_fwd(qkv_t, lengths)
    out_t, gmid_t, gatt_t, gg_two, gw_o, gw_gu, gw_dt = ffn(x_t, att_t, ct_t, gain_two, w_o, w_gu, w_dt, lengths)
    half = width // 2
    gw_gu = reduce_all(gw_gu.reshape(2, half, 2 * ff), 0, (2, 2, 2, 1, 1, 1))[0]
    gw_dt = reduce_all(gw_dt, 1, (0, 0, 0, 0, 0, 0))
    gw_o = reduce_all(gw_o.reshape(2, nq // 2, width), 0, (1, 1, 1, 2, 2, 1))[0]
    gq, gk, gv = att_bwd(qkv_t, gatt_t, att_t, lse, lengths, cos, sin)
    gx_t, gg_one, gw_qkv = post(x_t, gq, gk, gv, gmid_t, gain_one, w_qkv)
    gw_qkv = reduce_all(gw_qkv.reshape(2, half, nq + 2 * nkv), 0, (1, 1, 1, 2, 2, 1))[0]
    gg = reduce_small(jnp.concatenate([gg_one, gg_two], 1))

    totals = (
        gw_qkv[:, :nq].astype(F32),
        gw_qkv[:, nq:].reshape(half, 2, nkv).astype(F32),
        gw_o.astype(F32),
        gw_gu.reshape(half, 2, ff).astype(F32),
        gw_dt.T.astype(F32),
        gg,
    )
    shards = (w_query, w_keyval, w_output, w_gateup, w_down, gains)
    states = (state_query, state_keyval, state_output, state_gateup, state_down, state_gains)
    weights = tuple(weight.astype(F32) for weight in shards)
    squares_g, squares_w, entry_counts = ([], [], [])
    for weight, gradient, stacked in zip(weights, totals, STACKED):
        squares_g.extend(matrix_squares(gradient, stacked))
        squares_w.extend(matrix_squares(weight, stacked))
        entry_counts.extend([entries * 2 for entries in matrix_counts(weight, stacked)])
    sums = jnp.stack(squares_g + squares_w)
    sums = sums + swap(sums, "shard", 0)
    sums_g, sums_w = sums[:9], sums[9:]
    grad_scale = lax.rsqrt(sums_g / jnp.array(entry_counts, dtype=F32) + 1e-06)
    firsts, seconds, directions, squares_r = ([], [], [], [])
    start = 0
    for weight, gradient, state, stacked in zip(weights, totals, states, STACKED):
        normed_grad = gradient * spread_factor(grad_scale, start, weight, stacked)
        start = start + (2 if stacked else 1)
        first_moment = STATE_DECAY * state[0] + (1.0 - STATE_DECAY) * normed_grad
        second_moment = STATE_DECAY * state[1] + (1.0 - STATE_DECAY) * normed_grad * normed_grad
        direction = first_moment / (jnp.sqrt(second_moment) + 1e-06) + WEIGHT_DECAY * weight
        firsts.append(first_moment)
        seconds.append(second_moment)
        directions.append(direction)
        squares_r.extend(matrix_squares(direction, stacked))
    sums_r = jnp.stack(squares_r)
    sums_r = sums_r + swap(sums_r, "shard", 0)
    weight_norms = jnp.sqrt(sums_w)
    update_norms = jnp.sqrt(sums_r)
    trust_ratios = weight_norms * lax.rsqrt(sums_r + 1e-06)
    masters, new_states, copies = ([], [], [])
    start = 0
    for weight, direction, first_moment, second_moment, stacked in zip(weights, directions, firsts, seconds, STACKED):
        factor = spread_factor(trust_ratios, start, weight, stacked)
        start = start + (2 if stacked else 1)
        master = weight - LEARN_RATE * factor * direction
        masters.append(master)
        copies.append(master.astype(BF))
        new_states.append(jnp.stack([first_moment, second_moment]))
    return (
        jnp.swapaxes(out_t, 1, 2),
        jnp.swapaxes(gx_t, 1, 2),
        *totals,
        *new_states,
        *masters,
        *copies,
        weight_norms,
        update_norms,
        trust_ratios,
    )


def solution(mesh):
    in_specs = (
        P(("shard", "rep"), None, None),
        P(("shard", "rep"), None, None),
        P(("shard", "rep")),
        P("shard", None),
        P("shard", None, None),
        P("shard", None),
        P("shard", None, None),
        P("shard", None),
        P("shard", None),
        P(None, "shard", None),
        P(None, "shard", None, None),
        P(None, "shard", None),
        P(None, "shard", None, None),
        P(None, "shard", None),
        P(None, "shard", None),
    )
    out_specs = (
        P(("shard", "rep"), None, None),
        P(("shard", "rep"), None, None),
        P("shard", None),
        P("shard", None, None),
        P("shard", None),
        P("shard", None, None),
        P("shard", None),
        P("shard", None),
        P(None, "shard", None),
        P(None, "shard", None, None),
        P(None, "shard", None),
        P(None, "shard", None, None),
        P(None, "shard", None),
        P(None, "shard", None),
        P("shard", None),
        P("shard", None, None),
        P("shard", None),
        P("shard", None, None),
        P("shard", None),
        P("shard", None),
        P("shard", None),
        P("shard", None, None),
        P("shard", None),
        P("shard", None, None),
        P("shard", None),
        P("shard", None),
        P(),
        P(),
        P(),
    )
    return jax.shard_map(local, mesh=mesh, in_specs=in_specs, out_specs=out_specs, check_vma=False)
```

time: 1030 us -> 521 us (0.51)
  matrix products: 341 us -> 0 us
  waiting for transfers between devices: 277 us -> 101 us
  Pallas kernels: 0 us -> 148 us
  other arithmetic: 202 us -> 110 us
  blocking collectives: 99.5 us -> 24.6 us
  starting transfers between devices: 1.26 us -> 62.8 us
  local copies, waits for them, and re-layouts: 83 us -> 54 us
    dot_general x40 -> x0, matrix products: 339 us -> none  [the longest x2 53.6 us: attend_back(): jnp.einsum('qkgd,ckd->kgqc', grad_mixed, values_in, preferred_element_typ...]
    reduce_scatter x10 -> x0, waiting for transfers between devices: 150 us -> none  [the longest x2 98.2 us: local(): lax.psum_scatter(weight_grads[3].astype(jnp.bfloat16), 'shard', scatter_d...]
    pallas_call x0 -> x5, Pallas kernels: none -> 148 us  [the longest x1 72.3 us: ffn(): pl.pallas_call(functools.partial(ffn_kernel, rows=rows, chunk=chunk), gri...]
    psum x1 -> x0, waiting for transfers between devices: 126 us -> none  [local(): totals = lax.psum(owned, 'rep')]
    ppermute x0 -> x43, waiting for transfers between devices: none -> 69.4 us  [swap(): lax.ppermute(v, axis, [(i, i ^ 1 << bit) for i in range(lax.axis_size(axi...]
    convert_element_type x18 -> x30, other arithmetic: 83.5 us -> 19 us  [the longest x5 10.1 us: local(): copies.append(master.astype(BF))]
    ppermute x0 -> x43, starting transfers between devices: none -> 62.6 us  [swap(): lax.ppermute(v, axis, [(i, i ^ 1 << bit) for i in range(lax.axis_size(axi...]
    psum x3 -> x0, blocking collectives: 45.5 us -> none  [the longest x1 34.4 us: local(): totals = lax.psum(owned, 'rep')]
  transfers between devices with their start and end apart: 15 -> 46, of which waited for: 5 -> 28; matrix products, arithmetic and copies ran while one was open for 29% -> 14% of each run, Pallas kernels for 0% -> 8%
where the time goes in v1:
time: 521 us; the launch traced here: 517 us
  Pallas kernels  148 us (28%)
  other arithmetic  110 us (21%)
  waiting for transfers between devices  101 us (19%)
  starting transfers between devices  62.8 us (12%)
  local copies, waits for them, and re-layouts  54 us (10%)
  blocking collectives  24.6 us (5%)
  between operations  17.1 us (3%)
    pallas_call x1, Pallas kernels, ffn(): pl.pallas_call(functools.partial(ffn_kernel, rows=rows, chunk=chunk), gri...  72.3 us
    ppermute x43, waiting for transfers between devices, swap(): lax.ppermute(v, axis, [(i, i ^ 1 << bit) for i in range(lax.axis_size(axi...  69.4 us
    ppermute x43, starting transfers between devices, swap(): lax.ppermute(v, axis, [(i, i ^ 1 << bit) for i in range(lax.axis_size(axi...  62.6 us
    pallas_call x1, Pallas kernels, att_fwd(): pl.pallas_call(functools.partial(att_fwd_kernel, blk=blk), grid_spec=pltp...  33.9 us
    all_gather x3, waiting for transfers between devices, local(): gather = lambda v, dim: lax.all_gather(v, 'shard', axis=dim, tiled=True)  30.6 us
    pallas_call x1, Pallas kernels, att_bwd(): pl.pallas_call(functools.partial(att_bwd_kernel, blk=blk), grid_spec=pltp...  26.4 us
    all_gather x2, blocking collectives, local(): gather = lambda v, dim: lax.all_gather(v, 'shard', axis=dim, tiled=True)  24.6 us
    reduce_sum x9, other arithmetic, matrix_squares(): jnp.sum(tensor[:, 1] * tensor[:, 1])  19.3 us
  transfers between devices with their start and end apart: 46, of which 28 were waited for; matrix products, arithmetic and copies ran while one was open for 14% of the time, Pallas kernels for 8%

profile of v1, /device:TPU:0, one launch (start us, length us, event | category | flops | bytes accessed | tf_op | source)
XLA Modules:
  0.0 517.2 jit_solution(5529636764972819878)
XLA Ops:
  17.1 5.3 %all-gather = bf16[2,288,2]{1,2,0:T(2,128)(2,1)S(1)} all-gather(bf16[1,288,2]{1,2,0:T(2,128)(2,1)S(1)} %bitcast.176), channel_id=1, replica_groups=mesh['shard'=2,'rep'=16] {'shard'}, dimensions={0}, use_global_device_ids=true | all-gather | bytes 3456 | tf_op jit(solution)/shard_map/all_gather | solution.py:476
  24.7 19.2 %all_gather.17.wo_ref = bf16[576,576]{1,0:T(8,128)(2,1)} all-gather(bf16[288,576]{1,0:T(8,128)(2,1)S(1)} %copy-done.31), channel_id=1, replica_groups=mesh['shard'=2,'rep'=16] {'shard'}, dimensions={0}, use_global_device_ids=true | all-gather | bytes 995328 | tf_op jit(solution)/shard_map/all_gather | solution.py:476
  47.3 4.5 fusion.12
  53.2 5.2 pre_attention.1.q_ref.k_ref.v_ref
  58.4 33.9 %attention_forward.1 = (bf16[2,576,1024]{2,1,0:T(8,128)(2,1)S(1)}, f32[2,3,3,1024]{3,2,1,0:T(4,128)S(1)}) custom-call(s32[2]{0:T(128)S(1)} %copy-done.16, bf16[2,960,1024]{2,1,0:T(8,128)(2,1)S(1)} %pre_attention.1.q_ref.k_ref.v_ref, bf16[2,960,1024]{2,1,0:T(8,128)(2,1)S(1)} %pre_attention.1.q_ref.k_ref.v_ref, ...), custom_call_target="tpu_custom_call" | custom-call | tf_op jit(solution)/shard_map/attention_forward/pallas_call | solution.py:116
  95.5 30.6 %all-gather.7.cloned.1.call-done.wgu_ref = bf16[576,3072]{1,0:T(8,128)(2,1)} async-done(((bf16[288,3072]{1,0:T(8,128)(2,1)}), bf16[576,3072]{1,0:T(8,128)(2,1)}) %all-gather.7.cloned.1.call-update) | async-done | bytes 3538960 | tf_op jit(solution)/shard_map/all_gather | solution.py:476
  126.2 72.3 %feed_forward.1 = (bf16[2,576,1024]{2,1,0:T(8,128)(2,1)}, f32[2,576,1024]{2,1,0:T(8,128)}, bf16[2,576,1024]{2,1,0:T(8,128)(2,1)}, f32[576,1]{1,0:T(8,128)}, bf16...) custom-call(s32[2]{0:T(128)} %len_ref.5, bf16[2,576,1024]{2,1,0:T(8,128)(2,1)} %bitcast.141, ...), custom_call_target="tpu_custom_call" | custom-call | tf_op jit(solution)/shard_map/feed_forward/pallas_call | solution.py:320
  203.4 26.4 %attention_backward.1 = (bf16[2,576,1024]{2,1,0:T(8,128)(2,1)S(1)}, bf16[2,192,1024]{2,1,0:T(8,128)(2,1)S(1)}, bf16[2,192,1024]{2,1,0:T(8,128)(2,1)S(1)}) custom-call(s32[2]{0:T(128)S(1)} %copy-done.17, bf16[2,960,1024]{2,1,0:T(8,128)(2,1)S(1)} %copy-done.1, bf16[2,960,1024]{2,1,0:T(8,128)(2,1)S(1)} %copy-done.1, bf16[2,960,1024]{2,1,0:T(8,128)(2,1)S(1)} %copy-done.1, ...), custom_call_target="tpu_custom_call" | custom-call | tf_op jit(solution)/shard_map/attention_backward/pallas_call | solution.py:193
  232.9 10.3 %post_attention.1 = (bf16[2,576,1024]{2,1,0:T(8,128)(2,1)}, f32[576,1]{1,0:T(8,128)S(1)}, bf16[576,960]{1,0:T(8,128)(2,1)S(1)}) custom-call(bf16[2,576,1024]{2,1,0:T(8,128)(2,1)S(1)} %bitcast.143, bf16[2,576,1024]{2,1,0:T(8,128)(2,1)S(1)} %copy-done.11, bf16[2,192,1024]{2,1,0:T(8,128)(2,1)S(1)} %get-tuple-element.49.gk_ref, ...), custom_call_target="tpu_custom_call" | custom-call | tf_op jit(solution)/shard_map/post_attention/pallas_call | solution.py:384
  245.0 5.2 collective-permute-start.36
  253.7 8.0 %collective-permute-start.38 = (f32[288,2]{0,1:T(2,128)S(1)}, f32[288,2]{0,1:T(2,128)S(1)}, u32[]{:S(2)}, u32[]{:S(2)}) collective-permute-start(f32[288,2]{0,1:T(2,128)S(1)} %fusion.70), channel_id=1, source_target_pairs={{0,2},{1,3},{2,0},{3,1},{4,6},{5,7},{6,4},{7,5},{8,10},{9,11},{10,... | collective-permute-start | bytes 6920 | tf_op jit(solution)/shard_map/ppermute | solution.py:407
  266.9 3.9 collective-permute-start.40
  280.5 3.9 collective-permute-start.13
  329.2 13.0 %collective-permute-done.19 = bf16[1,288,1536]{2,1,0:T(8,128)(2,1)S(1)} collective-permute-done((bf16[1,288,1536]{2,1,0:T(8,128)(2,1)S(1)}, bf16[1,288,1536]{2,1,0:T(8,128)(2,1)S(1)}, u32[]{:S(2)}, u32[]{:S(2)}) %collective-permute-start.19) | collective-permute-done | bytes 884768 | tf_op jit(solution)/shard_map/ppermute | solution.py:407
  345.9 4.9 collective-permute-done.20
  353.6 5.8 %collective-permute-done.21 = bf16[1,288,384]{2,1,0:T(8,128)(2,1)S(1)} collective-permute-done((bf16[1,288,384]{2,1,0:T(8,128)(2,1)S(1)}, bf16[1,288,384]{2,1,0:T(8,128)(2,1)S(1)}, u32[]{:S(2)}, u32[]{:S(2)}) %collective-permute-start.21) | collective-permute-done | bytes 221216 | tf_op jit(solution)/shard_map/ppermute | solution.py:407
  362.5 4.2 collective-permute-done.22
  368.7 3.9 collective-permute-done.23
  375.2 3.5 collective-permute-done.24
  382.4 4.7 collective-permute-done.25
  398.9 4.6 reshape.1491
  403.5 4.3 fusion.10
  407.8 11.4 %stack.147 = f32[18]{0:T(128)S(1)} concatenate(f32[1]{0:T(128)} %bitcast.31, f32[1]{0:T(128)} %bitcast.32, f32[1]{0:T(128)} %bitcast.33, f32[1]{0:T(128)} %bitcast.34, f32[1]{0:T(128)} %bitcast.35, f32[1]{0:T(128)} %bitcast.36, f32[1]{0:T(128)} %bitcast.37, f32[1]{0:T(128)} %bitcast.38, f32[1]{0:T(128)} %bitcast.39, f32[1]{0:T(128)} %bitcast.40, f32[1]{0:T(128)} %bitcast.41, ...), dimensions={0} | concatenate | bytes 144 | tf_op jit(solution)/shard_map/stack | solution.py:513
  419.9 3.7 copy.110
  429.2 11.1 %multiply_add_fusion.2 = f32[288,2,1536]{2,1,0:T(2,128)S(1)} fusion(f32[288,2,1536]{2,1,0:T(2,128)S(1)} %reshape.1491, f32[2,288,2,1536]{3,2,1,0:T(2,128)} %param.30, f32[2]{0:T(128)S(1)} %get-tuple-element.215, bf16[288,2,1536]{2,1,0:T(2,128)(2,1)S(1)} %copy-done.22), kind=kLoop, calls=%fused_computation.12 | loop fusion | flops 10616832 | bytes 15925256 | tf_op jit(solution)/shard_map/add | solution.py:524
  440.3 4.5 fusion.14
  448.8 4.9 multiply_reduce_fusion
  456.3 6.0 %stack.169 = f32[9]{0:T(128)S(1)} concatenate(f32[1]{0:T(128)} %bitcast.68, f32[1]{0:T(128)} %bitcast.71, f32[1]{0:T(128)} %bitcast.72, f32[1]{0:T(128)} %bitcast.75, f32[1]{0:T(128)} %bitcast.78, f32[1]{0:T(128)} %bitcast.79, f32[1]{0:T(128)} %bitcast.80, f32[1]{0:T(128)} %bitcast.81, f32[1]{0:T(128)} %bitcast.82), dimensions={0} | concatenate | bytes 72 | tf_op jit(solution)/shard_map/stack | solution.py:529
  466.6 14.0 %multiply_add_fusion.1 = (f32[1,288,2,1536]{3,2,1,0:T(2,128)}, f32[1,288,2,1536]{3,2,1,0:T(2,128)}) fusion(f32[2,288,2,1536]{3,2,1,0:T(2,128)} %param.30, f32[2]{0:T(128)S(1)} %get-tuple-element.215, bf16[1,288,1,1536]{3,2,1,0:T(2,128)(2,1)S(1)} %copy-done.27, bf16[1,288,1,1536]{3,2,1,0:T(2,128)(2,1)} %copy.110, pred[]{:T(512)S(6)} %eq.8), kind=kLoop, calls=%fused_computation.4 | loop fusion | flops 15040512 | bytes 15925257 | tf_op jit(solution)/shard_map/add | solution.py:522
  480.6 9.4 %pad_maximum_fusion = f32[2,288,2,1536]{3,2,1,0:T(2,128)} fusion(f32[1,288,2,1536]{3,2,1,0:T(2,128)} %get-tuple-element.194, f32[1,288,2,1536]{3,2,1,0:T(2,128)} %get-tuple-element.193), kind=kLoop, calls=%fused_computation | loop fusion | flops 1769472 | bytes 14155776 | tf_op jit(solution)/shard_map/stack | solution.py:542
  490.0 3.6 pad_maximum_fusion.1
  501.0 4.8 fusion.57
  (334 shorter events, 149.1 us)
Async XLA Ops:
  7.2 44.5 %all-gather.5.cloned.1.call-start = ((), (), s32[]{:S(2)}) async-start(), calls=%async_computation | async-start | bytes 1769472 | tf_op jit(solution)/shard_map/all_gather | solution.py:476
  10.5 85.0 %all-gather.9.cloned.1.call-start = ((), (), s32[]{:S(2)}) async-start(), calls=%async_computation.2 | async-start | bytes 2654208 | tf_op jit(solution)/shard_map/all_gather | solution.py:476
  11.3 114.9 %all-gather.7.cloned.1.call-start = ((), (), s32[]{:S(2)}) async-start(), calls=%async_computation.1 | async-start | bytes 5308416 | tf_op jit(solution)/shard_map/all_gather | solution.py:476
  245.0 6.9 %collective-permute-start.36 = (f32[288,2]{0,1:T(2,128)}, f32[288,2]{0,1:T(2,128)S(1)}, u32[]{:S(2)}, u32[]{:S(2)}) collective-permute-start(f32[288,2]{0,1:T(2,128)} %fusion.47), channel_id=1, source_target_pairs={{0,16},{16,0},{1,17},{17,1},{2,18},{18,2},{3,19},{19,3},{4,20},{20... | collective-permute-start | bytes 6920 | tf_op jit(solution)/shard_map/ppermute | solution.py:407
  253.1 10.2 %collective-permute-start.9 = (bf16[2,144,576]{2,1,0:T(8,128)(2,1)S(1)}, bf16[2,144,576]{2,1,0:T(8,128)(2,1)S(1)}, u32[]{:S(2)}, u32[]{:S(2)}) collective-permute-start(bf16[2,144,576]{2,1,0:T(8,128)(2,1)S(1)} %constant_dynamic-slice_fusion.18), channel_id=1, source_target_pairs={{0,1},{1,0},{2,3},{3,2},{4,5},{5,4},{6,7},{7,6},{8,9},{9,8},{10,11... | collective-permute-start | bytes 995336 | tf_op jit(solution)/shard_map/ppermute | solution.py:407
  253.7 9.5 %collective-permute-start.38 = (f32[288,2]{0,1:T(2,128)S(1)}, f32[288,2]{0,1:T(2,128)S(1)}, u32[]{:S(2)}, u32[]{:S(2)}) collective-permute-start(f32[288,2]{0,1:T(2,128)S(1)} %fusion.70), channel_id=1, source_target_pairs={{0,2},{1,3},{2,0},{3,1},{4,6},{5,7},{6,4},{7,5},{8,10},{9,11},{10,... | collective-permute-start | bytes 6920 | tf_op jit(solution)/shard_map/ppermute | solution.py:407
  262.8 21.6 %collective-permute-start = (bf16[2,144,960]{2,1,0:T(8,128)(2,1)S(1)}, bf16[2,144,960]{2,1,0:T(8,128)(2,1)S(1)}, u32[]{:S(2)}, u32[]{:S(2)}) collective-permute-start(bf16[2,144,960]{2,1,0:T(8,128)(2,1)S(1)} %constant_dynamic-slice_fusion.23), channel_id=1, source_target_pairs={{0,1},{1,0},{2,3},{3,2},{4,5},{5,4},{6,7},{7,6},{8,9},{9,8},{10,11... | collective-permute-start | bytes 1658888 | tf_op jit(solution)/shard_map/ppermute | solution.py:407
  264.4 7.0 %collective-permute-start.10 = (bf16[1,144,576]{2,1,0:T(8,128)(2,1)S(1)}, bf16[1,144,576]{2,1,0:T(8,128)(2,1)S(1)}, u32[]{:S(2)}, u32[]{:S(2)}) collective-permute-start(bf16[1,144,576]{2,1,0:T(8,128)(2,1)S(1)} %constant_dynamic-slice_fusion.17), channel_id=1, source_target_pairs={{0,16},{16,0},{1,17},{17,1},{2,18},{18,2},{3,19},{19,3},{4,20},{20... | collective-permute-start | bytes 497672 | tf_op jit(solution)/shard_map/ppermute | solution.py:407
  266.6 53.2 %collective-permute-start.18 = (bf16[2,288,1536]{2,1,0:T(8,128)(2,1)S(1)}, bf16[2,288,1536]{2,1,0:T(8,128)(2,1)S(1)}, u32[]{:S(2)}, u32[]{:S(2)}) collective-permute-start(bf16[2,288,1536]{2,1,0:T(8,128)(2,1)S(1)} %constant_dynamic-slice_fusion.13), channel_id=1, source_target_pairs={{0,1},{1,0},{2,3},{3,2},{4,5},{5,4},{6,7},{7,6},{8,9},{9,8},{10,11... | collective-permute-start | bytes 5308424 | tf_op jit(solution)/shard_map/ppermute | solution.py:407
  266.9 6.2 %collective-permute-start.40 = (f32[288,2]{0,1:T(2,128)S(1)}, f32[288,2]{0,1:T(2,128)S(1)}, u32[]{:S(2)}, u32[]{:S(2)}) collective-permute-start(f32[288,2]{0,1:T(2,128)S(1)} %add.351), channel_id=1, source_target_pairs={{0,8},{1,9},{2,10},{3,11},{4,12},{5,13},{6,14},{7,15},{8,0},{9,1},... | collective-permute-start | bytes 6920 | tf_op jit(solution)/shard_map/ppermute | solution.py:407
  273.0 36.6 %collective-permute-start.27 = (bf16[288,1536]{1,0:T(8,128)(2,1)S(1)}, bf16[288,1536]{1,0:T(8,128)(2,1)S(1)}, u32[]{:S(2)}, u32[]{:S(2)}) collective-permute-start(bf16[288,1536]{1,0:T(8,128)(2,1)S(1)} %constant_dynamic-slice_fusion.8), channel_id=1, source_target_pairs={{0,1},{1,0},{2,3},{3,2},{4,5},{5,4},{6,7},{7,6},{8,9},{9,8},{10,11... | collective-permute-start | bytes 2654216 | tf_op jit(solution)/shard_map/ppermute | solution.py:407
  280.5 5.8 %collective-permute-start.13 = (bf16[1,36,288]{2,1,0:T(8,128)(2,1)S(1)}, bf16[1,36,288]{2,1,0:T(8,128)(2,1)S(1)}, u32[]{:S(2)}, u32[]{:S(2)}) collective-permute-start(bf16[1,36,288]{2,1,0:T(8,128)(2,1)S(1)} %constant_dynamic-slice_fusion.14), channel_id=1, source_target_pairs={{0,8},{1,9},{2,10},{3,11},{4,12},{5,13},{6,14},{7,15},{8,0},{9,1},... | collective-permute-start | bytes 62216 | tf_op jit(solution)/shard_map/ppermute | solution.py:407
  289.4 7.2 %collective-permute-start.1 = (bf16[1,144,960]{2,1,0:T(8,128)(2,1)S(1)}, bf16[1,144,960]{2,1,0:T(8,128)(2,1)S(1)}, u32[]{:S(2)}, u32[]{:S(2)}) collective-permute-start(bf16[1,144,960]{2,1,0:T(8,128)(2,1)S(1)} %constant_dynamic-slice_fusion.22), channel_id=1, source_target_pairs={{0,16},{16,0},{1,17},{17,1},{2,18},{18,2},{3,19},{19,3},{4,20},{20... | collective-permute-start | bytes 829448 | tf_op jit(solution)/shard_map/ppermute | solution.py:407
  300.2 23.0 %collective-permute-start.17 = (bf16[1,144,576]{2,1,0:T(8,128)(2,1)S(1)}, bf16[1,144,576]{2,1,0:T(8,128)(2,1)S(1)}, u32[]{:S(2)}, u32[]{:S(2)}) collective-permute-start(bf16[1,144,576]{2,1,0:T(8,128)(2,1)S(1)} %maximum_select_fusion.16), channel_id=1, source_target_pairs={{0,1},{1,0},{2,3},{3,2},{4,5},{5,4},{6,7},{7,6},{8,9},{9,8},{10,11... | collective-permute-start | bytes 497672 | tf_op jit(solution)/shard_map/ppermute | solution.py:407
  314.7 13.2 %collective-permute-start.28 = (bf16[288,768]{1,0:T(8,128)(2,1)S(1)}, bf16[288,768]{1,0:T(8,128)(2,1)S(1)}, u32[]{:S(2)}, u32[]{:S(2)}) collective-permute-start(bf16[288,768]{1,0:T(8,128)(2,1)S(1)} %constant_dynamic-slice_fusion.7), channel_id=1, source_target_pairs={{0,16},{16,0},{1,17},{17,1},{2,18},{18,2},{3,19},{19,3},{4,20},{20... | collective-permute-start | bytes 1327112 | tf_op jit(solution)/shard_map/ppermute | solution.py:407
  320.5 21.7 %collective-permute-start.19 = (bf16[1,288,1536]{2,1,0:T(8,128)(2,1)S(1)}, bf16[1,288,1536]{2,1,0:T(8,128)(2,1)S(1)}, u32[]{:S(2)}, u32[]{:S(2)}) collective-permute-start(bf16[1,288,1536]{2,1,0:T(8,128)(2,1)S(1)} %constant_dynamic-slice_fusion.12), channel_id=1, source_target_pairs={{0,16},{16,0},{1,17},{17,1},{2,18},{18,2},{3,19},{19,3},{4,20},{20... | collective-permute-start | bytes 2654216 | tf_op jit(solution)/shard_map/ppermute | solution.py:407
  327.5 18.3 %collective-permute-start.8 = (bf16[1,144,960]{2,1,0:T(8,128)(2,1)S(1)}, bf16[1,144,960]{2,1,0:T(8,128)(2,1)S(1)}, u32[]{:S(2)}, u32[]{:S(2)}) collective-permute-start(bf16[1,144,960]{2,1,0:T(8,128)(2,1)S(1)} %maximum_select_fusion.11), channel_id=1, source_target_pairs={{0,1},{1,0},{2,3},{3,2},{4,5},{5,4},{6,7},{7,6},{8,9},{9,8},{10,11... | collective-permute-start | bytes 829448 | tf_op jit(solution)/shard_map/ppermute | solution.py:407
  328.0 15.7 %collective-permute-start.29 = (bf16[144,768]{1,0:T(8,128)(2,1)S(1)}, bf16[144,768]{1,0:T(8,128)(2,1)S(1)}, u32[]{:S(2)}, u32[]{:S(2)}) collective-permute-start(bf16[144,768]{1,0:T(8,128)(2,1)S(1)} %constant_dynamic-slice_fusion.6), channel_id=1, source_target_pairs={{0,2},{1,3},{2,0},{3,1},{4,6},{5,7},{6,4},{7,5},{8,10},{9,11},{10,... | collective-permute-start | bytes 663560 | tf_op jit(solution)/shard_map/ppermute | solution.py:407
  342.5 8.4 %collective-permute-start.20 = (bf16[1,288,768]{2,1,0:T(8,128)(2,1)S(1)}, bf16[1,288,768]{2,1,0:T(8,128)(2,1)S(1)}, u32[]{:S(2)}, u32[]{:S(2)}) collective-permute-start(bf16[1,288,768]{2,1,0:T(8,128)(2,1)S(1)} %constant_dynamic-slice_fusion.11), channel_id=1, source_target_pairs={{0,2},{1,3},{2,0},{3,1},{4,6},{5,7},{6,4},{7,5},{8,10},{9,11},{10,... | collective-permute-start | bytes 1327112 | tf_op jit(solution)/shard_map/ppermute | solution.py:407
  343.8 9.2 %collective-permute-start.30 = (bf16[72,768]{1,0:T(8,128)(2,1)S(1)}, bf16[72,768]{1,0:T(8,128)(2,1)S(1)}, u32[]{:S(2)}, u32[]{:S(2)}) collective-permute-start(bf16[72,768]{1,0:T(8,128)(2,1)S(1)} %constant_dynamic-slice_fusion.5), channel_id=1, source_target_pairs={{0,4},{1,5},{2,6},{3,7},{4,0},{5,1},{6,2},{7,3},{8,12},{9,13},{10,... | collective-permute-start | bytes 331784 | tf_op jit(solution)/shard_map/ppermute | solution.py:407
  351.0 8.3 %collective-permute-start.21 = (bf16[1,288,384]{2,1,0:T(8,128)(2,1)S(1)}, bf16[1,288,384]{2,1,0:T(8,128)(2,1)S(1)}, u32[]{:S(2)}, u32[]{:S(2)}) collective-permute-start(bf16[1,288,384]{2,1,0:T(8,128)(2,1)S(1)} %constant_dynamic-slice_fusion.10), channel_id=1, source_target_pairs={{0,4},{1,5},{2,6},{3,7},{4,0},{5,1},{6,2},{7,3},{8,12},{9,13},{10,... | collective-permute-start | bytes 663560 | tf_op jit(solution)/shard_map/ppermute | solution.py:407
  353.0 7.1 %collective-permute-start.31 = (bf16[36,768]{1,0:T(8,128)(2,1)S(1)}, bf16[36,768]{1,0:T(8,128)(2,1)S(1)}, u32[]{:S(2)}, u32[]{:S(2)}) collective-permute-start(bf16[36,768]{1,0:T(8,128)(2,1)S(1)} %constant_dynamic-slice_fusion.4), channel_id=1, source_target_pairs={{0,8},{1,9},{2,10},{3,11},{4,12},{5,13},{6,14},{7,15},{8,0},{9,1},... | collective-permute-start | bytes 165896 | tf_op jit(solution)/shard_map/ppermute | solution.py:407
  359.4 7.3 %collective-permute-start.22 = (bf16[1,144,384]{2,1,0:T(8,128)(2,1)S(1)}, bf16[1,144,384]{2,1,0:T(8,128)(2,1)S(1)}, u32[]{:S(2)}, u32[]{:S(2)}) collective-permute-start(bf16[1,144,384]{2,1,0:T(8,128)(2,1)S(1)} %constant_dynamic-slice_fusion.9), channel_id=1, source_target_pairs={{0,8},{1,9},{2,10},{3,11},{4,12},{5,13},{6,14},{7,15},{8,0},{9,1},... | collective-permute-start | bytes 331784 | tf_op jit(solution)/shard_map/ppermute | solution.py:407
  360.1 7.6 %collective-permute-start.32 = (bf16[36,768]{1,0:T(8,128)(2,1)S(1)}, bf16[36,768]{1,0:T(8,128)(2,1)S(1)}, u32[]{:S(2)}, u32[]{:S(2)}) collective-permute-start(bf16[36,768]{1,0:T(8,128)(2,1)S(1)} %add_convert_fusion.16), channel_id=1, source_target_pairs={{0,8},{1,9},{2,10},{3,11},{4,12},{5,13},{6,14},{7,15},{8,0},{9,1},... | collective-permute-start | bytes 165896 | tf_op jit(solution)/shard_map/ppermute | solution.py:407
  366.8 5.8 %collective-permute-start.23 = (bf16[1,144,384]{2,1,0:T(8,128)(2,1)S(1)}, bf16[1,144,384]{2,1,0:T(8,128)(2,1)S(1)}, u32[]{:S(2)}, u32[]{:S(2)}) collective-permute-start(bf16[1,144,384]{2,1,0:T(8,128)(2,1)S(1)} %add_convert_fusion.13), channel_id=1, source_target_pairs={{0,8},{1,9},{2,10},{3,11},{4,12},{5,13},{6,14},{7,15},{8,0},{9,1},... | collective-permute-start | bytes 331784 | tf_op jit(solution)/shard_map/ppermute | solution.py:407
  367.7 5.9 %collective-permute-start.33 = (bf16[72,768]{1,0:T(8,128)(2,1)S(1)}, bf16[72,768]{1,0:T(8,128)(2,1)S(1)}, u32[]{:S(2)}, u32[]{:S(2)}) collective-permute-start(bf16[72,768]{1,0:T(8,128)(2,1)S(1)} %maximum_select_fusion.19), channel_id=1, source_target_pairs={{0,4},{1,5},{2,6},{3,7},{4,0},{5,1},{6,2},{7,3},{8,12},{9,13},{10,... | collective-permute-start | bytes 331784 | tf_op jit(solution)/shard_map/ppermute | solution.py:407
  372.6 6.0 %collective-permute-start.24 = (bf16[1,288,384]{2,1,0:T(8,128)(2,1)S(1)}, bf16[1,288,384]{2,1,0:T(8,128)(2,1)S(1)}, u32[]{:S(2)}, u32[]{:S(2)}) collective-permute-start(bf16[1,288,384]{2,1,0:T(8,128)(2,1)S(1)} %maximum_select_fusion.13), channel_id=1, source_target_pairs={{0,4},{1,5},{2,6},{3,7},{4,0},{5,1},{6,2},{7,3},{8,12},{9,13},{10,... | collective-permute-start | bytes 663560 | tf_op jit(solution)/shard_map/ppermute | solution.py:407
  373.7 8.4 %collective-permute-start.34 = (bf16[144,768]{1,0:T(8,128)(2,1)S(1)}, bf16[144,768]{1,0:T(8,128)(2,1)S(1)}, u32[]{:S(2)}, u32[]{:S(2)}) collective-permute-start(bf16[144,768]{1,0:T(8,128)(2,1)S(1)} %maximum_select_fusion.14), channel_id=1, source_target_pairs={{0,2},{1,3},{2,0},{3,1},{4,6},{5,7},{6,4},{7,5},{8,10},{9,11},{10,... | collective-permute-start | bytes 663560 | tf_op jit(solution)/shard_map/ppermute | solution.py:407
  378.8 8.4 %collective-permute-start.25 = (bf16[1,288,768]{2,1,0:T(8,128)(2,1)S(1)}, bf16[1,288,768]{2,1,0:T(8,128)(2,1)S(1)}, u32[]{:S(2)}, u32[]{:S(2)}) collective-permute-start(bf16[1,288,768]{2,1,0:T(8,128)(2,1)S(1)} %maximum_select_fusion.6), channel_id=1, source_target_pairs={{0,2},{1,3},{2,0},{3,1},{4,6},{5,7},{6,4},{7,5},{8,10},{9,11},{10,... | collective-permute-start | bytes 1327112 | tf_op jit(solution)/shard_map/ppermute | solution.py:407
  382.2 8.2 %collective-permute-start.35 = (bf16[288,768]{1,0:T(8,128)(2,1)S(1)}, bf16[288,768]{1,0:T(8,128)(2,1)S(1)}, u32[]{:S(2)}, u32[]{:S(2)}) collective-permute-start(bf16[288,768]{1,0:T(8,128)(2,1)S(1)} %maximum_select_fusion.7), channel_id=1, source_target_pairs={{0,1},{1,0},{2,3},{3,2},{4,5},{5,4},{6,7},{7,6},{8,9},{9,8},{10,11... | collective-permute-start | bytes 1327112 | tf_op jit(solution)/shard_map/ppermute | solution.py:407
  387.4 8.3 %collective-permute-start.26 = (bf16[1,288,1536]{2,1,0:T(8,128)(2,1)S(1)}, bf16[1,288,1536]{2,1,0:T(8,128)(2,1)S(1)}, u32[]{:S(2)}, u32[]{:S(2)}) collective-permute-start(bf16[1,288,1536]{2,1,0:T(8,128)(2,1)S(1)} %maximum_select_fusion.1), channel_id=1, source_target_pairs={{0,1},{1,0},{2,3},{3,2},{4,5},{5,4},{6,7},{7,6},{8,9},{9,8},{10,11... | collective-permute-start | bytes 2654216 | tf_op jit(solution)/shard_map/ppermute | solution.py:407
  462.3 34.7 %collective-permute-start.42 = (f32[9]{0:T(128)S(1)}, f32[9]{0:T(128)S(1)}, u32[]{:S(2)}, u32[]{:S(2)}) collective-permute-start(f32[9]{0:T(128)S(1)} %stack.169), channel_id=1, source_target_pairs={{0,16},{16,0},{1,17},{17,1},{2,18},{18,2},{3,19},{19,3},{4,20},{20... | collective-permute-start | bytes 116 | tf_op jit(solution)/shard_map/ppermute | solution.py:407
  (82 other events, 877.8 us)
Sparse Core Ops, SparseCore 0:
  10.7 33.2 all-gather.4
  45.5 29.0 all-gather.8
  76.8 49.3 all-gather.6
